TPU v7x, 32 devices: a whole 2x2x4 slice. The times are simulated.
32 devices in a mesh: group: 4 (over y, core), local: 8 (over z, x).
Axes of the slice: x: 2, y: 2, z: 4, core: 2. Of those that a mesh axis runs over, the one named last changes fastest.
Arguments:
- hidden_states: bfloat16 [4096, 3584], P(('group', 'local')), may hold values from -6 to 6
- affinity: float32 [4096, 8], P(('group', 'local')), may hold values from 0.1 to 1
- group_ids: int32 [4096, 4], P(('group', 'local')), may hold values from 0 to 3, as said below
- expert_ids: int32 [4096, 8], P(('group', 'local')), may hold values from 0 to 31, as said below
- w_gate: bfloat16 [32, 3584, 1024], P(('group', 'local')), may hold values from -0.09375 to 0.09375
- w_up: bfloat16 [32, 3584, 1024], P(('group', 'local')), may hold values from -0.09375 to 0.09375
- w_down: bfloat16 [32, 1024, 3584], P(('group', 'local')), may hold values from -0.1875 to 0.1875
Outputs:
- routed_out: bfloat16 [4096, 3584], P(('group', 'local'))
Inputs may be any that keep to these rules, and one draw needn't show every extreme that they name: `group_ids`: each row names 4 different groups, and every group is named by exactly 128 of the tokens of one device. `expert_ids`: each row names 8 different experts; columns 2 j and 2 j + 1 lie in group group_ids[t, j]. Of the tokens of one device at most 40 name any one expert, and in every group some expert is named by exactly 40 tokens of every device.
All inputs are finite; a program needn't handle non-finite values.
Results may differ from a plain program's by a relative error of at most 0.007.
Values may be sent and summed in bfloat16 or wider, within the bound.
No kernel may reach another device: no remote copies, remote signals or barrier semaphores. Data moves between devices by JAX's collectives and lax.ppermute only.
A program may use at most 128 MiB of HBM per device.

v0:
```python
import jax
import jax.numpy as jnp
from jax import lax
from jax.sharding import PartitionSpec as P

TOP_K = 8
TOPG = 4


def expert_apply(received, gate_mat, up_mat, down_mat):
    shape_in = received.shape
    rows_in = received.reshape(-1, shape_in[-1])
    gate_act = jnp.dot(rows_in, gate_mat, preferred_element_type=jnp.float32)
    up_act = jnp.dot(rows_in, up_mat, preferred_element_type=jnp.float32)
    hidden = (jax.nn.silu(gate_act) * up_act).astype(jnp.bfloat16)
    produced = jnp.dot(hidden, down_mat, preferred_element_type=jnp.float32).astype(jnp.bfloat16)
    return produced.reshape(shape_in)


def shards(hidden_states, affinity, group_ids, expert_ids, w_gate, w_up, w_down):
    tok_rows = hidden_states.shape[0]
    model_width = hidden_states.shape[1]
    group_count = lax.axis_size("group")
    local_count = lax.axis_size("local")
    experts_all = group_count * local_count
    most_rows = 5 * tok_rows * TOP_K // (4 * experts_all)
    pair_size = TOP_K // TOPG
    zero_row = jnp.zeros((), jnp.bfloat16)
    gate_weights = (2.5 * affinity / jnp.sum(affinity, axis=1, keepdims=True)).astype(jnp.bfloat16)
    chosen = jnp.repeat(group_ids, pair_size, axis=1)
    is_valid = expert_ids // local_count == chosen
    mixing = jnp.where(is_valid, gate_weights, zero_row)
    target = jnp.where(is_valid, expert_ids, experts_all)
    member = jnp.sum(
        (target[:, :, None] == jnp.arange(experts_all)[None, None, :]).astype(jnp.int32), axis=1
    )
    before = jnp.cumsum(member, axis=0) - member
    is_slot = (member.T[:, None, :] > 0) & (
        before.T[:, None, :] == jnp.arange(most_rows)[None, :, None]
    )
    source = jnp.sum(jnp.where(is_slot, jnp.arange(tok_rows)[None, None, :], 0), axis=2)
    filled = jnp.any(is_slot, axis=2)
    outgoing = jnp.where(filled[:, :, None], hidden_states[source], zero_row)
    results = lax.all_to_all(
        expert_apply(
            lax.all_to_all(outgoing, ("group", "local"), split_axis=0, concat_axis=0, tiled=True),
            w_gate[0],
            w_up[0],
            w_down[0],
        ),
        ("group", "local"),
        split_axis=0,
        concat_axis=0,
        tiled=True,
    )
    safe_ids = jnp.minimum(target, experts_all - 1)
    slot_pos = safe_ids * most_rows + jnp.take_along_axis(before, safe_ids, axis=1)
    picked = results.reshape(-1, model_width)[slot_pos]
    group_part = jnp.einsum(
        "tgk,tgkd->tgd",
        mixing.reshape(tok_rows, TOPG, pair_size),
        picked.reshape(tok_rows, TOPG, pair_size, model_width),
        preferred_element_type=jnp.float32,
    ).astype(jnp.bfloat16)
    group_part = lax.optimization_barrier(group_part)
    return jnp.sum(group_part.astype(jnp.float32), axis=1).astype(jnp.bfloat16)


def solution(mesh):
    placed = (
        P(("group", "local"), None),
        P(("group", "local"), None),
        P(("group", "local"), None),
        P(("group", "local"), None),
        P(("group", "local"), None, None),
        P(("group", "local"), None, None),
        P(("group", "local"), None, None),
    )
    return jax.shard_map(
        shards, mesh=mesh, in_specs=placed, out_specs=P(("group", "local"), None), check_vma=False
    )
```

profile of v0, /device:TPU:0, one launch (start us, length us, event | category | flops | bytes accessed | tf_op | source)
XLA Modules:
  0.0 527.0 jit_solution(12237393922358794127)
XLA Ops:
  0.0 0.8 broadcast_in_dim.51
  0.8 0.7 bitcast_or_fusion
  1.5 0.1 copy.28
  1.6 0.2 reduce_window_sum.11
  1.8 0.6 select_reduce_fusion
  2.5 0.6 fusion.8
  3.2 7.9 %gather_fusion = bf16[1280,3584]{1,0:T(8,128)(2,1)} fusion(bf16[128,3584]{1,0:T(8,128)(2,1)S(1)} %copy-done, s32[2048]{0:T(1024)S(1)} %pad_clamp_fusion), kind=kCustom, calls=%fused_computation | custom fusion | bytes 18355200 | tf_op jit(solution)/shard_map/gather | solution.py:43
  11.2 7.8 %broadcast_select_fusion = bf16[32,40,3584]{2,1,0:T(8,128)(2,1)} fusion(bf16[32,40,3584]{2,1,0:T(8,128)(2,1)} %bitcast.39, pred[32,40]{1,0:T(8,128)(4,1)S(1)} %fusion.8), kind=kLoop, calls=%fused_computation.4 | loop fusion | flops 4587520 | bytes 18351360 | tf_op jit(solution)/shard_map/jit(_where)/select_n | solution.py:43
  19.0 209.0 %all_to_all.10 = bf16[32,40,3584]{2,1,0:T(8,128)(2,1)S(1)} all-to-all(bf16[32,40,3584]{2,1,0:T(8,128)(2,1)} %broadcast_select_fusion), channel_id=1, replica_groups=mesh['group'=4,'local'=8] {'group','local'}, dimensions={0} | all-to-all | bytes 18350080 | tf_op jit(solution)/shard_map/all_to_all | solution.py:46
  228.1 9.7 %fusion.1 = f32[1280,1024]{1,0:T(8,128)S(1)} fusion(bf16[1280,3584]{1,0:T(8,128)(2,1)S(1)} %bitcast.42, bf16[1,3584,1024]{2,1,0:T(8,128)(2,1)S(1)} %copy-done.3), kind=kOutput, calls=%fused_computation.7 | convolution fusion | flops 9395240960 | bytes 21757952 | tf_op jit(solution)/shard_map/dot_general | solution.py:14
  237.7 12.7 %multiply_convert_fusion = bf16[1280,1024]{1,0:T(8,128)(2,1)S(1)} fusion(f32[1280,1024]{1,0:T(8,128)S(1)} %fusion.1, bf16[1280,3584]{1,0:T(8,128)(2,1)S(1)} %bitcast.43, bf16[1,3584,1024]{2,1,0:T(8,128)(2,1)} %param.11), kind=kOutput, calls=%fused_computation.11 | convolution fusion | flops 9403105280 | bytes 24379392 | tf_op jit(solution)/shard_map/dot_general | solution.py:13
  250.5 15.0 %convolution_convert_fusion = bf16[1280,3584]{1,0:T(8,128)(2,1)} fusion(bf16[1280,1024]{1,0:T(8,128)(2,1)S(1)} %multiply_convert_fusion, bf16[1,1024,3584]{2,1,0:T(8,128)(2,1)} %param.13), kind=kOutput, calls=%fused_computation.3 | convolution fusion | flops 9399828480 | bytes 19136512 | tf_op jit(solution)/shard_map/dot_general | solution.py:16
  265.5 3.7 all-to-all-start.1
  269.2 0.1 copy.31
  269.4 7.1 %gather_fusion.2 = s32[1024]{0:T(1024)S(1)} fusion(s32[128,32]{1,0:T(8,128)S(1)} %sub.14, s32[1024]{0:T(1024)S(1)} %reshape.69), kind=kCustom, calls=%fused_computation.2 | custom fusion | bytes 16384 | tf_op jit(solution)/shard_map/jit(take_along_axis)/gather | solution.py:57
  276.6 0.1 copy.33
  276.8 0.1 reshape.63
  276.9 0.2 copy.34
  277.1 195.2 %all-to-all-done.1 = bf16[32,40,3584]{2,1,0:T(8,128)(2,1)} async-done(((bf16[32,40,3584]{2,1,0:T(8,128)(2,1)}), bf16[32,40,3584]{2,1,0:T(8,128)(2,1)}, u32[]{:S(2)}, u32[]{:S(2)}) %all-to-all-start.1) | async-done | bytes 9175072 | tf_op jit(solution)/shard_map/all_to_all | solution.py:44
  472.3 18.6 %gather_fusion.1 = bf16[1024,3584]{1,0:T(8,128)(2,1)} fusion(bf16[1280,3584]{1,0:T(8,128)(2,1)} %bitcast.12, s32[1024]{0:T(1024)S(1)} %broadcast_clamp_fusion), kind=kCustom, calls=%fused_computation.1 | custom fusion | bytes 14684160 | tf_op jit(solution)/shard_map/gather | solution.py:58
  490.9 14.9 %reshape.52 = bf16[128,4,2,3584]{3,2,1,0:T(2,128)(2,1)} reshape(bf16[1024,3584]{1,0:T(8,128)(2,1)} %gather_fusion.1) | data formatting | bytes 14680064 | tf_op jit(solution)/shard_map/reshape | solution.py:62
  505.8 10.1 %fusion.14 = bf16[128,4,1,3584]{3,2,1,0:T(2,128)(2,1)S(1)} fusion(bf16[128,4,2,1]{2,3,1,0:T(2,128)(2,1)S(1)} %copy.34, bf16[128,4,2,3584]{3,2,1,0:T(2,128)(2,1)} %reshape.52), kind=kOutput, calls=%fused_computation.36 | convolution fusion | flops 7340032 | bytes 11012096 | tf_op jit(solution)/shard_map/tgk,tgkd->tgd/dot_general | solution.py:59
  515.9 3.7 copy.37
  519.6 7.4 %reduce_sum.45 = bf16[128,3584]{1,0:T(8,128)(2,1)} reduce(bf16[128,4,3584]{2,1,0:T(4,128)(2,1)} %bitcast.40, bf16[]{:T(256)} %constant.49.clone.1), dimensions={1}, to_apply=%region_5.6 | reduce | flops 1376256 | bytes 4587522 | tf_op jit(solution)/shard_map/reduce_sum | solution.py:66
  (22 shorter events, 0.5 us)
Async XLA Ops:
  0.0 3.2 copy-start
  19.0 209.1 %copy-start.3 = (bf16[1,3584,1024]{2,1,0:T(8,128)(2,1)S(1)}, bf16[1,3584,1024]{2,1,0:T(8,128)(2,1)}, u32[]{:S(2)}) copy-start(bf16[1,3584,1024]{2,1,0:T(8,128)(2,1)} %param.12) | copy-start | bytes 22020100
  265.5 206.8 %all-to-all-start.1 = ((bf16[32,40,3584]{2,1,0:T(8,128)(2,1)}), bf16[32,40,3584]{2,1,0:T(8,128)(2,1)}, u32[]{:S(2)}, u32[]{:S(2)}) async-start(bf16[32,40,3584]{2,1,0:T(8,128)(2,1)} %bitcast.41), calls=%async_computation.1 | async-start | bytes 18350080 | tf_op jit(solution)/shard_map/all_to_all | solution.py:44
  269.4 7.5 %copy-start.2 = (f32[128,8]{0,1:T(8,128)S(1)}, f32[128,8]{0,1:T(8,128)}, u32[]{:S(2)}) copy-start(f32[128,8]{0,1:T(8,128)} %param.8) | copy-start | bytes 12292
  505.8 21.2 %copy-start.1 = (bf16[128,3584]{1,0:T(8,128)(2,1)S(1)}, bf16[128,3584]{1,0:T(8,128)(2,1)}, u32[]{:S(2)}) copy-start(bf16[128,3584]{1,0:T(8,128)(2,1)} %param.7) | copy-start | bytes 2752516
where the time goes:
time: 529 us; the launch traced here: 527 us
  blocking collectives  209 us (40%)
  waiting for transfers between devices  195 us (37%)
  local copies, waits for them, and re-layouts  53.9 us (10%)
  matrix products  47.5 us (9%)
  other arithmetic  17.5 us (3%)
    all_to_all x1, blocking collectives, shards(): lax.all_to_all(outgoing, ('group', 'local'), split_axis=0, concat_axis=0,...  209 us
    all_to_all x1, waiting for transfers between devices, shards(): lax.all_to_all(expert_apply(lax.all_to_all(outgoing, ('group', 'local'),...  195 us
    gather x1, local copies, waits for them, and re-layouts, shards(): picked = results.reshape(-1, model_width)[slot_pos]  18.6 us
    dot_general x1, matrix products, expert_apply(): jnp.dot(hidden, down_mat, preferred_element_type=jnp.float32)  15 us
    reshape x1, local copies, waits for them, and re-layouts, shards(): picked.reshape(tok_rows, TOPG, pair_size, model_width)  14.9 us
    dot_general x1, matrix products, expert_apply(): gate_act = jnp.dot(rows_in, gate_mat, preferred_element_type=jnp.float32)  12.7 us
  transfers between devices with their start and end apart: 1, of which 1 were waited for; matrix products, arithmetic and copies ran while one was open for 1% of the time, Pallas kernels for 0%

commit v1 on v0

v1 whole, which is shorter than its diff:
```python
import functools

import jax
import jax.numpy as jnp
from jax import lax
from jax.experimental import pallas as pl
from jax.experimental.pallas import tpu as pltpu
from jax.sharding import PartitionSpec as P

ALL = ("row", "core", "plane", "column")
PLANE = ("row", "core", "column")
META = 16
OFFSET = 1 << 20
SMALL = 24 * 1024 * 1024
LARGE = 52 * 1024 * 1024


def plan(mesh_shape):
    group_count, local_count = mesh_shape["group"], mesh_shape["local"]
    cores = 2
    planes = 1
    while planes * planes < local_count:
        planes *= 2
    return group_count // cores, cores, planes, local_count // planes


def swap(value, axis, delta):
    size = lax.axis_size(axis)
    return lax.ppermute(value, axis, [(i, i ^ delta) for i in range(size)])


def swap_in_plane(value, dx, dy):
    xs, ys = lax.axis_size("column"), lax.axis_size("row")
    cs = lax.axis_size("core")
    pairs = [
        ((y * cs + c) * xs + x, ((y ^ dy) * cs + c) * xs + (x ^ dx))
        for y in range(ys)
        for c in range(cs)
        for x in range(xs)
    ]
    return lax.ppermute(value, PLANE, pairs)


def tile_of(width, most):
    best = 128
    for size in range(128, most + 1, 128):
        if width % size == 0:
            best = size
    return best


def call(
    kernel, grid, in_specs, out_specs, out_shape, scratch, flops, nbytes, after, operands, limit
):
    return pl.pallas_call(
        kernel,
        grid=grid,
        in_specs=list(in_specs) + [pl.BlockSpec(memory_space=pl.ANY)] * len(after),
        out_specs=out_specs,
        out_shape=out_shape,
        scratch_shapes=scratch,
        cost_estimate=pl.CostEstimate(flops=flops, bytes_accessed=nbytes, transcendentals=0),
        compiler_params=pltpu.CompilerParams(
            dimension_semantics=("arbitrary",), vmem_limit_bytes=limit
        ),
    )(*operands, *after)


def select_kernel(top_k, parts, n_after, want_ref, *refs):
    tokens = refs[:4]
    rest = refs[4 + n_after :]
    outs, (weight_ref, pick) = rest[:parts], rest[parts:]
    step = pl.program_id(0)
    tok = tokens[0].shape[0] - META

    @pl.when(step == 0)
    def _():
        want = want_ref[...]
        rows_all = want.shape[0]
        for at, ref in enumerate(tokens[::2]):
            info = ref[tok : tok + META, : 3 * tok].astype(jnp.float32)
            code = info[:, :tok] * tok + info[:, tok : 2 * tok] + float(at * OFFSET)
            found = jnp.zeros((rows_all, tok), jnp.float32)
            weight = jnp.zeros((rows_all, tok), jnp.float32)
            for k in range(top_k):
                hit = code[k : k + 1, :] == want
                found = jnp.where(hit, 1.0, found)
                weight = jnp.where(hit, info[k : k + 1, 2 * tok :], weight)
            pick[:, at * tok : (at + 1) * tok] = found.astype(jnp.bfloat16)
            weight_ref[at * tok : (at + 1) * tok, :] = weight.T.astype(jnp.bfloat16)

    for half in range(2):

        @pl.when(step == half)
        def _():
            own, sib = tokens[half][:tok, :], tokens[2 + half][:tok, :]
            rows = jnp.dot(pick[:, :tok], own, preferred_element_type=jnp.float32)
            rows += jnp.dot(pick[:, tok:], sib, preferred_element_type=jnp.float32)
            rows = rows.astype(jnp.bfloat16)
            pair = outs[0].shape[0]
            for i, out in enumerate(outs):
                out[...] = rows[i * pair : (i + 1) * pair]


def select(want, own, sib, top_k, parts, after):
    rows_all = want.shape[0]
    tok, tile = own[0].shape[0] - META, own[0].shape[1]
    width = 2 * tile
    pair = rows_all // parts
    kernel = functools.partial(select_kernel, top_k, parts, len(after))
    *sent, weight = call(
        kernel,
        (2,),
        [pl.BlockSpec((rows_all, 1), lambda j: (0, 0))]
        + [pl.BlockSpec((tok + META, tile), lambda j: (0, 0))] * 4,
        [pl.BlockSpec((pair, tile), lambda j: (0, j))] * parts
        + [pl.BlockSpec((2 * tok, rows_all), lambda j: (0, 0))],
        [jax.ShapeDtypeStruct((pair, width), jnp.bfloat16)] * parts
        + [jax.ShapeDtypeStruct((2 * tok, rows_all), jnp.bfloat16)],
        [pltpu.VMEM((rows_all, 2 * tok), jnp.bfloat16)],
        4 * rows_all * tok * width,
        2 * width * (2 * tok + rows_all),
        after,
        (want, *own, *sib),
        SMALL,
    )
    return sent, weight


def expert_kernel(parts, first, n_after, *refs):
    rows, (gate_ref, up_ref, down_ref) = refs[:parts], refs[parts : parts + 3]
    rest = refs[parts + 3 + n_after :]
    outs, (rows_in, hidden) = rest[:parts], rest[parts:]
    step = pl.program_id(0)
    pair = rows[0].shape[0]
    tile = gate_ref.shape[2]

    @pl.when(step == 0)
    def _():
        for i in range(parts):
            rows_in[pl.ds(i * pair, pair), :] = rows[i][...]

    @pl.when(step < first)
    def _():
        data = rows_in[...]
        gate_act = jnp.dot(data, gate_ref[0], preferred_element_type=jnp.float32)
        up_act = jnp.dot(data, up_ref[0], preferred_element_type=jnp.float32)
        act = gate_act / (1.0 + jnp.exp(-gate_act)) * up_act
        for i in range(first):

            @pl.when(step == i)
            def _():
                hidden[:, i * tile : (i + 1) * tile] = act.astype(jnp.bfloat16)

    @pl.when(step >= first)
    def _():
        made = jnp.dot(hidden[...], down_ref[0], preferred_element_type=jnp.float32)
        made = made.astype(jnp.bfloat16)
        for i in range(parts):
            outs[i][...] = made[i * pair : (i + 1) * pair]


def expert(rows, w_gate, w_up, w_down, after):
    parts = len(rows)
    pair, width = rows[0].shape
    hid = w_gate.shape[2]
    tile_h, tile_w = tile_of(hid, 256), tile_of(width, 512)
    first = hid // tile_h
    second = width // tile_w
    kernel = functools.partial(expert_kernel, parts, first, len(after))

    def early(j):
        return (0, 0, jnp.minimum(j, first - 1))

    def late(j):
        return (0, 0, jnp.maximum(j - first, 0))

    return call(
        kernel,
        (first + second,),
        [pl.BlockSpec((pair, width), lambda j: (0, 0))] * parts
        + [
            pl.BlockSpec((1, width, tile_h), early),
            pl.BlockSpec((1, width, tile_h), early),
            pl.BlockSpec((1, hid, tile_w), late),
        ],
        [pl.BlockSpec((pair, tile_w), lambda j: (0, jnp.maximum(j - first, 0)))] * parts,
        [jax.ShapeDtypeStruct((pair, width), jnp.bfloat16)] * parts,
        [
            pltpu.VMEM((parts * pair, width), jnp.bfloat16),
            pltpu.VMEM((parts * pair, hid), jnp.bfloat16),
        ],
        6 * parts * pair * hid * width,
        6 * hid * width + 4 * parts * pair * width,
        after,
        (*rows, w_gate, w_up, w_down),
        LARGE,
    )


def combine_kernel(parts, n_after, weight_ref, *refs):
    home = refs[:parts]
    own_ref, left_ref, right_ref, rows = refs[parts + n_after :]
    step = pl.program_id(0)
    tok = own_ref.shape[0]
    pair = home[0].shape[0]
    for i in range(parts):
        rows[pl.ds(i * pair, pair), :] = home[i][...]
    mixed = jnp.dot(weight_ref[...], rows[...], preferred_element_type=jnp.float32)
    own_ref[...] = mixed[:tok]
    for half, sib_ref in enumerate((left_ref, right_ref)):

        @pl.when(step == half)
        def _():
            sib_ref[...] = mixed[tok:].astype(jnp.bfloat16)


def combine(weight, home, after):
    parts = len(home)
    both, rows_all = weight.shape
    tok = both // 2
    pair, width = home[0].shape
    tile = width // 2
    half = pl.BlockSpec((tok, tile), lambda j: (0, 0))
    return call(
        functools.partial(combine_kernel, parts, len(after)),
        (2,),
        [pl.BlockSpec((both, rows_all), lambda j: (0, 0))]
        + [pl.BlockSpec((pair, tile), lambda j: (0, j))] * parts,
        [pl.BlockSpec((tok, tile), lambda j: (0, j)), half, half],
        [jax.ShapeDtypeStruct((tok, width), jnp.float32)]
        + [jax.ShapeDtypeStruct((tok, tile), jnp.bfloat16)] * 2,
        [pltpu.VMEM((rows_all, tile), jnp.bfloat16)],
        2 * rows_all * both * width,
        2 * width * (both * 2 + rows_all),
        after,
        (weight, *home),
        SMALL,
    )


def pass_kernel(count, n_after, *refs):
    outs = refs[count + n_after :]
    for i in range(count):
        outs[i][...] = refs[i][...]


def passed(values, after):
    rows, width = values[0].shape
    tile = tile_of(width, width // 2)
    count = len(values)
    return call(
        functools.partial(pass_kernel, count, len(after)),
        (width // tile,),
        [pl.BlockSpec((rows, tile), lambda j: (0, j))] * count,
        [pl.BlockSpec((rows, tile), lambda j: (0, j))] * count,
        [jax.ShapeDtypeStruct(value.shape, value.dtype) for value in values],
        [],
        1,
        4 * count * rows * width,
        after,
        tuple(values),
        SMALL,
    )


def relay_kernel(chooser, copies, whole, count, n_after, plane_ref, *refs):
    step = pl.program_id(0)
    values = [ref[...] for ref in refs[:count]]
    left_ref, right_ref, *outs = refs[count + n_after :]
    kept = chooser(plane_ref[0], *values)
    for half, ref in enumerate((left_ref, right_ref)):

        @pl.when(step == half)
        def _():
            ref[...] = kept

    for value, out in zip([kept] * whole + values[:copies], outs):
        out[...] = value


def relay(chooser, plane, values, whole, copies, after):
    rows, width = values[0].shape
    tile = width // 2
    count = len(values)
    block = pl.BlockSpec((rows, tile), lambda j: (0, j))
    half = pl.BlockSpec((rows, tile), lambda j: (0, 0))
    return call(
        functools.partial(relay_kernel, chooser, copies, whole, count, len(after)),
        (2,),
        [pl.BlockSpec(memory_space=pltpu.SMEM)] + [block] * count,
        [half, half] + [block] * (whole + copies),
        [jax.ShapeDtypeStruct((rows, tile), jnp.bfloat16)] * 2
        + [jax.ShapeDtypeStruct((rows, width), jnp.bfloat16)] * (whole + copies),
        [],
        1,
        2 * (count + 1 + whole + copies) * rows * width,
        after,
        (plane, *values),
        SMALL,
    )


def add_kernel(n_after, own_ref, left_ref, right_ref, *rest):
    out_ref = rest[n_after]
    half = left_ref.shape[1]
    for at, ref in enumerate((left_ref, right_ref)):
        part = own_ref[:, at * half : (at + 1) * half] + ref[...].astype(jnp.float32)
        out_ref[:, at * half : (at + 1) * half] = part.astype(out_ref.dtype)


def added(own, sib, after):
    tok, width = own.shape
    half = pl.BlockSpec((tok, width // 2), lambda j: (0, 0))
    whole = pl.BlockSpec((tok, width), lambda j: (0, 0))
    return call(
        functools.partial(add_kernel, len(after)),
        (1,),
        [whole, half, half],
        whole,
        jax.ShapeDtypeStruct((tok, width), jnp.bfloat16),
        [],
        tok * width,
        8 * tok * width,
        after,
        (own, *sib),
        SMALL,
    )


def route(affinity, group_ids, expert_ids, experts_all, local_count):
    tok_rows, top_k = expert_ids.shape
    pair_size = top_k // group_ids.shape[1]
    gate_weights = (2.5 * affinity / jnp.sum(affinity, axis=1, keepdims=True)).astype(jnp.bfloat16)
    chosen = jnp.repeat(group_ids, pair_size, axis=1)
    is_valid = expert_ids // local_count == chosen
    mixing = jnp.where(is_valid, gate_weights, jnp.zeros((), jnp.bfloat16)).T
    target = jnp.where(is_valid, expert_ids, -1).T
    is_member = target[:, None, :] == jnp.arange(experts_all)[None, :, None]
    member = jnp.sum(is_member.astype(jnp.float32), axis=0).astype(jnp.bfloat16)
    earlier = (jnp.arange(tok_rows)[:, None] < jnp.arange(tok_rows)[None, :]).astype(jnp.bfloat16)
    before = jnp.dot(member, earlier, preferred_element_type=jnp.float32)
    slot = jnp.sum(jnp.where(is_member, before[None], 0.0), axis=1)
    info = [target.astype(jnp.bfloat16), slot.astype(jnp.bfloat16), mixing]
    return jnp.pad(jnp.concatenate(info, axis=1), ((0, META - top_k), (0, 0)))


def shards(dims, hidden_states, affinity, group_ids, expert_ids, w_gate, w_up, w_down):
    ys, cs, zs, xs = dims
    tok_rows, width = hidden_states.shape
    top_k = expert_ids.shape[1]
    local_count = zs * xs
    experts_all = ys * cs * local_count
    most_rows = 5 * tok_rows * top_k // (4 * experts_all)
    me_y, me_c = lax.axis_index("row"), lax.axis_index("core")
    me_z, me_x = lax.axis_index("plane"), lax.axis_index("column")
    plane = me_z.astype(jnp.int32).reshape(1)

    meta = route(affinity, group_ids, expert_ids, experts_all, local_count)
    meta = jnp.pad(meta, ((0, 0), (0, width - meta.shape[1])))
    payload = jnp.concatenate([hidden_states, meta], axis=0)
    middle = width // 2
    payload_halves = [
        jnp.concatenate([hidden_states[:, :middle], meta[:, :middle]], axis=0),
        jnp.concatenate([hidden_states[:, middle:], meta[:, middle:]], axis=0),
    ]

    rel = [(dx, dy) for dx in range(xs) for dy in range(ys)]
    parts = len(rel)
    pair = -(-cs * most_rows // 16) * 16
    wanted = jnp.stack(
        [((me_y ^ dy) * cs + me_c) * local_count + me_z * xs + (me_x ^ dx) for dx, dy in rel]
    ).astype(jnp.float32)
    row = jnp.arange(pair)
    in_pair = jnp.where(
        row < cs * most_rows, row // most_rows * OFFSET + row % most_rows, -2 * OFFSET
    ).astype(jnp.float32)
    want = (wanted[:, None] * tok_rows + in_pair[None, :]).reshape(-1, 1)

    tokens, siblings, arrived, weights, made, halves, sums = {}, {}, {}, {}, {}, {}, {}
    last = []

    def hop(value, step, sources):
        return lax.ppermute(value, "plane", [(z, z + step) for z in sources])

    def have(dz, halves):
        tokens[dz] = halves
        siblings[dz] = [swap(half, "core", 1) for half in halves]

    def relayed(dz, chooser, values, whole, copies, *after):
        left, right, *outs = relay(chooser, plane, values, whole, copies, last + list(after))
        last[:] = [left]
        have(dz, (left, right))
        return outs

    def in_plane(values):
        return [
            part if (dx, dy) == (0, 0) else swap_in_plane(part, dx, dy)
            for part, (dx, dy) in zip(values, rel)
        ]

    def dispatch(dz, *after):
        sent, weights[dz] = select(
            want, tokens[dz], siblings[dz], top_k, parts, last + list(after)
        )
        last[:] = [weights[dz]]
        arrived[dz] = in_plane(sent)

    def apply(dz, *after):
        made[dz] = expert(arrived[dz], w_gate, w_up, w_down, last + list(after))
        last[:] = [made[dz][0]]

    def give_back(dz, late=False):
        sent = made[dz]
        if late:
            sent = passed(sent, last)
            last[:] = [sent[0]]
        halves[dz] = in_plane(sent)

    def collect(dz, *after):
        own, *sib = combine(weights[dz], halves[dz], last + list(after))
        last[:] = [sib[0]]
        halves[dz] = own, [swap(half, "core", 1) for half in sib]

    def send_home(dz, *after):
        part = added(*halves[dz], last + list(after))
        last[:] = [part]
        sums[dz] = swap(part, "plane", dz)

    up1, down1 = hop(payload, 1, (0, 1, 2)), hop(payload, -1, (1, 2, 3))
    have(0, payload_halves)
    dispatch(0)
    up1, down1 = relayed(
        1, lambda z, u, d: jnp.where(z % 2 == 1, u, d), [up1, down1], 0, 2, *arrived[0]
    )
    up2, down2 = hop(up1, 1, (1, 2)), hop(down1, -1, (1, 2))
    dispatch(1)
    apply(0)
    (second,) = relayed(
        2, lambda z, u, d: jnp.where(z >= 2, u, d), [up2, down2], 1, 0, *arrived[1]
    )
    ends = lax.ppermute(second, "plane", [(1, 0), (2, 3)])
    dispatch(2)
    apply(1)
    relayed(
        3,
        lambda z, u, d, e: jnp.where(z == 1, d, jnp.where(z == 2, u, e)),
        [up1, down1, ends],
        0,
        0,
        *arrived[2],
    )
    dispatch(3)
    apply(2)
    give_back(2)
    apply(3)
    give_back(3)
    collect(2)
    send_home(2)
    give_back(1, late=True)
    collect(3)
    send_home(3, sums[2])
    give_back(0, late=True)
    collect(1)
    send_home(1, sums[3])
    collect(0)
    own, sib = halves[0]
    sums[0] = own + jnp.concatenate(sib, axis=1).astype(jnp.float32)
    total = sums[0]
    for dz in range(1, zs):
        total = total + sums[dz].astype(jnp.float32)
    return total.astype(jnp.bfloat16)


def solution(mesh):
    dims = plan(mesh.shape)
    finer = jax.sharding.Mesh(mesh.devices.reshape(dims), ALL)

    def body(*args):
        return shards(dims, *args)

    placed = (P(ALL, None),) * 4 + (P(ALL, None, None),) * 3
    return jax.shard_map(body, mesh=finer, in_specs=placed, out_specs=P(ALL, None), check_vma=False)
```

time: 529 us -> 286 us (0.54)
  blocking collectives: 209 us -> 0 us
  Pallas kernels: 0 us -> 88.8 us
  waiting for transfers between devices: 195 us -> 120 us
  starting transfers between devices: 3.68 us -> 67.2 us
  local copies, waits for them, and re-layouts: 53.9 us -> 3.72 us
  matrix products: 47.5 us -> 0.14 us
  other arithmetic: 17.5 us -> 4.89 us
    all_to_all x1 -> x0, blocking collectives: 209 us -> none  [shards(): lax.all_to_all(outgoing, ('group', 'local'), split_axis=0, concat_axis=0,...]
    all_to_all x1 -> x0, waiting for transfers between devices: 195 us -> none  [shards(): lax.all_to_all(expert_apply(lax.all_to_all(outgoing, ('group', 'local'),...]
    ppermute x0 -> x48, waiting for transfers between devices: none -> 120 us  [the longest x19 57.4 us: swap(): return lax.ppermute(value, axis, [(i, i ^ delta) for i in range(size)])]
    pallas_call x0 -> x20, Pallas kernels: none -> 88.8 us  [call(): pl.pallas_call(kernel, grid=grid, in_specs=list(in_specs) + [pl.BlockSpec...]
    ppermute x0 -> x48, starting transfers between devices: none -> 67.2 us  [the longest x24 28.9 us: swap_in_plane(): return lax.ppermute(value, PLANE, pairs)]
    dot_general x4 -> x1, matrix products: 47.5 us -> 0.14 us  [route(): before = jnp.dot(member, earlier, preferred_element_type=jnp.float32)]
    gather x7 -> x0, local copies, waits for them, and re-layouts: 33.9 us -> none  [the longest x1 18.6 us: shards(): picked = results.reshape(-1, model_width)[slot_pos]]
    reshape x2 -> x0, local copies, waits for them, and re-layouts: 15.1 us -> none  [the longest x1 14.9 us: shards(): picked.reshape(tok_rows, TOPG, pair_size, model_width)]
  transfers between devices with their start and end apart: 1 -> 48, of which waited for: 1 -> 24; matrix products, arithmetic and copies ran while one was open for 1% -> 0% of each run, Pallas kernels for 0% -> 30%
where the time goes in v1:
time: 286 us; the launch traced here: 285 us
  waiting for transfers between devices  120 us (42%)
  Pallas kernels  88.8 us (31%)
  starting transfers between devices  67.2 us (23%)
  other arithmetic  4.89 us (2%)
  local copies, waits for them, and re-layouts  3.72 us (1%)
    pallas_call x20, Pallas kernels, call(): pl.pallas_call(kernel, grid=grid, in_specs=list(in_specs) + [pl.BlockSpec...  88.8 us
    ppermute x19, waiting for transfers between devices, swap(): return lax.ppermute(value, axis, [(i, i ^ delta) for i in range(size)])  57.4 us
    ppermute x24, waiting for transfers between devices, swap_in_plane(): return lax.ppermute(value, PLANE, pairs)  38.9 us
    ppermute x24, starting transfers between devices, swap_in_plane(): return lax.ppermute(value, PLANE, pairs)  28.9 us
    ppermute x19, starting transfers between devices, swap(): return lax.ppermute(value, axis, [(i, i ^ delta) for i in range(size)])  27.9 us
    ppermute x4, waiting for transfers between devices, hop(): return lax.ppermute(value, 'plane', [(z, z + step) for z in sources])  20.4 us
    ppermute x4, starting transfers between devices, hop(): return lax.ppermute(value, 'plane', [(z, z + step) for z in sources])  8.91 us
  transfers between devices with their start and end apart: 48, of which 24 were waited for; matrix products, arithmetic and copies ran while one was open for 0% of the time, Pallas kernels for 30%

profile of v1, /device:TPU:0, one launch (start us, length us, event | category | flops | bytes accessed | tf_op | source)
XLA Modules:
  0.0 285.4 jit_solution(18004564817971943939)
XLA Ops:
  7.4 5.6 %collective-permute-start.5 = (bf16[144,3584]{1,0:T(8,128)(2,1)}, bf16[144,3584]{1,0:T(8,128)(2,1)S(1)}, u32[]{:S(2)}, u32[]{:S(2)}) collective-permute-start(bf16[144,3584]{1,0:T(8,128)(2,1)} %pad_maximum_fusion), channel_id=1, source_target_pairs={{0,2},{2,4},{4,6},{1,3},{3,5},{5,7},{8,10},{10,12},{12,14},{9,11},... | collective-permute-start | bytes 3096584 | tf_op jit(solution)/shard_map/ppermute | solution.py:384
  13.4 3.2 %shard_map.73 = (bf16[80,3584]{1,0:T(8,128)(2,1)S(1)}, bf16[80,3584]{1,0:T(8,128)(2,1)S(1)}, bf16[80,3584]{1,0:T(8,128)(2,1)S(1)}, bf16[80,3584]{1,0:T(8,128)(2,1)S(1)}, bf16[256,320]{1,0:T(8,128)(2,1)S(1)}) custom-call(f32[320,1]{1,0:T(8,128)S(1)} %add.110.want_ref, bf16[144,1792]{1,0:T(8,128)(2,1)S(1)} %pad_maximum_fusion.1.refs_0_, ...), custom_call_target="tpu_custom_call" | custom-call | flops 587202560 | bytes 4128768 | tf_op jit(solution)/shard_map/pallas_call | solution.py:55
  16.6 2.0 collective-permute-start.2
  20.2 14.0 %collective-permute-done.6.refs_1_ = bf16[144,3584]{1,0:T(8,128)(2,1)S(1)} collective-permute-done((bf16[144,3584]{1,0:T(8,128)(2,1)}, bf16[144,3584]{1,0:T(8,128)(2,1)S(1)}, u32[]{:S(2)}, u32[]{:S(2)}) %collective-permute-start.6) | collective-permute-done | bytes 1032224 | tf_op jit(solution)/shard_map/ppermute | solution.py:384
  35.5 9.3 %collective-permute-done.4.refs_6_.refs_3_ = bf16[80,3584]{1,0:T(8,128)(2,1)S(1)} collective-permute-done((bf16[80,3584]{1,0:T(8,128)(2,1)S(1)}, bf16[80,3584]{1,0:T(8,128)(2,1)S(1)}, u32[]{:S(2)}, u32[]{:S(2)}) %collective-permute-start.4) | collective-permute-done | bytes 573472 | tf_op jit(solution)/shard_map/ppermute | solution.py:41
  48.3 2.0 shard_map.75
  53.8 17.2 %shard_map.76 = (bf16[80,3584]{1,0:T(8,128)(2,1)S(1)}, bf16[80,3584]{1,0:T(8,128)(2,1)S(1)}, bf16[80,3584]{1,0:T(8,128)(2,1)S(1)}, bf16[80,3584]{1,0:T(8,128)(2,1)}) custom-call(bf16[80,3584]{1,0:T(8,128)(2,1)} %copy-done.1, bf16[80,3584]{1,0:T(8,128)(2,1)} %copy-done.4, bf16[80,3584]{1,0:T(8,128)(2,1)} %copy-done.7, bf16[80,3584]{1,0:T(8,128)(2,1)} %copy-done.10, ...), custom_call_target="tpu_custom_call" | custom-call | flops 7046430720 | bytes 26607616 | tf_op jit(solution)/shard_map/pallas_call | solution.py:55
  71.0 5.0 %collective-permute-done.10.refs_1_ = bf16[144,3584]{1,0:T(8,128)(2,1)S(1)} collective-permute-done((bf16[144,3584]{1,0:T(8,128)(2,1)S(1)}, bf16[144,3584]{1,0:T(8,128)(2,1)S(1)}, u32[]{:S(2)}, u32[]{:S(2)}) %collective-permute-start.10) | collective-permute-done | bytes 1032224 | tf_op jit(solution)/shard_map/ppermute | solution.py:384
  76.1 2.7 collective-permute-done.13.refs_6_.refs_3_
  82.3 2.7 shard_map.78
  88.5 17.2 %shard_map.79 = (bf16[80,3584]{1,0:T(8,128)(2,1)S(1)}, bf16[80,3584]{1,0:T(8,128)(2,1)S(1)}, bf16[80,3584]{1,0:T(8,128)(2,1)S(1)}, bf16[80,3584]{1,0:T(8,128)(2,1)}) custom-call(bf16[80,3584]{1,0:T(8,128)(2,1)} %copy-done, bf16[80,3584]{1,0:T(8,128)(2,1)} %copy-done.3, bf16[80,3584]{1,0:T(8,128)(2,1)} %copy-done.5, bf16[80,3584]{1,0:T(8,128)(2,1)} %copy-done.8, ...), custom_call_target="tpu_custom_call" | custom-call | flops 7046430720 | bytes 26607616 | tf_op jit(solution)/shard_map/pallas_call | solution.py:55
  105.7 3.4 %collective-permute-done.14.refs_2_ = bf16[144,3584]{1,0:T(8,128)(2,1)S(1)} collective-permute-done((bf16[144,3584]{1,0:T(8,128)(2,1)S(1)}, bf16[144,3584]{1,0:T(8,128)(2,1)S(1)}, u32[]{:S(2)}, u32[]{:S(2)}) %collective-permute-start.14) | collective-permute-done | bytes 1032224 | tf_op jit(solution)/shard_map/ppermute | solution.py:442
  109.2 4.5 %collective-permute-done.19.refs_7_.refs_3_ = bf16[80,3584]{1,0:T(8,128)(2,1)S(1)} collective-permute-done((bf16[80,3584]{1,0:T(8,128)(2,1)S(1)}, bf16[80,3584]{1,0:T(8,128)(2,1)S(1)}, u32[]{:S(2)}, u32[]{:S(2)}) %collective-permute-start.19) | collective-permute-done | bytes 573472 | tf_op jit(solution)/shard_map/ppermute | solution.py:41
  117.2 2.0 shard_map.81
  122.7 17.2 %shard_map.82 = (bf16[80,3584]{1,0:T(8,128)(2,1)S(1)}, bf16[80,3584]{1,0:T(8,128)(2,1)S(1)}, bf16[80,3584]{1,0:T(8,128)(2,1)S(1)}, bf16[80,3584]{1,0:T(8,128)(2,1)}) custom-call(bf16[80,3584]{1,0:T(8,128)(2,1)} %copy-done.2, bf16[80,3584]{1,0:T(8,128)(2,1)} %copy-done.6, bf16[80,3584]{1,0:T(8,128)(2,1)} %copy-done.9, bf16[80,3584]{1,0:T(8,128)(2,1)} %copy-done.11, ...), custom_call_target="tpu_custom_call" | custom-call | flops 7046430720 | bytes 26607616 | tf_op jit(solution)/shard_map/pallas_call | solution.py:55
  144.2 4.8 %collective-permute-done.24.refs_3_ = bf16[80,3584]{1,0:T(8,128)(2,1)} collective-permute-done((bf16[80,3584]{1,0:T(8,128)(2,1)S(1)}, bf16[80,3584]{1,0:T(8,128)(2,1)}, u32[]{:S(2)}, u32[]{:S(2)}) %collective-permute-start.24) | collective-permute-done | bytes 573472 | tf_op jit(solution)/shard_map/ppermute | solution.py:41
  149.0 17.3 %shard_map.83 = (bf16[80,3584]{1,0:T(8,128)(2,1)S(1)}, bf16[80,3584]{1,0:T(8,128)(2,1)S(1)}, bf16[80,3584]{1,0:T(8,128)(2,1)S(1)}, bf16[80,3584]{1,0:T(8,128)(2,1)}) custom-call(bf16[80,3584]{1,0:T(8,128)(2,1)} %copy-done.16, bf16[80,3584]{1,0:T(8,128)(2,1)} %copy-done.18, bf16[80,3584]{1,0:T(8,128)(2,1)} %copy-done.19, ...), custom_call_target="tpu_custom_call" | custom-call | flops 7046430720 | bytes 26607616 | tf_op jit(solution)/shard_map/pallas_call | solution.py:55
  169.8 3.7 %collective-permute-done.30.refs_3_ = bf16[80,3584]{1,0:T(8,128)(2,1)S(1)} collective-permute-done((bf16[80,3584]{1,0:T(8,128)(2,1)}, bf16[80,3584]{1,0:T(8,128)(2,1)S(1)}, u32[]{:S(2)}, u32[]{:S(2)}) %collective-permute-start.30) | collective-permute-done | bytes 573472 | tf_op jit(solution)/shard_map/ppermute | solution.py:41
  177.9 6.1 %collective-permute-start.35 = (bf16[128,3584]{1,0:T(8,128)(2,1)S(1)}, bf16[128,3584]{1,0:T(8,128)(2,1)S(1)}, u32[]{:S(2)}, u32[]{:S(2)}) collective-permute-start(bf16[128,3584]{1,0:T(8,128)(2,1)S(1)} %shard_map.85.refs_4_), channel_id=1, source_target_pairs={{0,4},{2,6},{4,0},{6,2},{1,5},{3,7},{5,1},{7,3},{8,12},{10,14},{12... | collective-permute-start | bytes 2752520 | tf_op jit(solution)/shard_map/ppermute | solution.py:29
  186.0 11.0 %collective-permute-done.27.refs_3_ = bf16[80,3584]{1,0:T(8,128)(2,1)S(1)} collective-permute-done((bf16[80,3584]{1,0:T(8,128)(2,1)}, bf16[80,3584]{1,0:T(8,128)(2,1)S(1)}, u32[]{:S(2)}, u32[]{:S(2)}) %collective-permute-start.27) | collective-permute-done | bytes 573472 | tf_op jit(solution)/shard_map/ppermute | solution.py:41
  203.1 21.1 %collective-permute-done.35.rest_1_ = bf16[128,3584]{1,0:T(8,128)(2,1)S(1)} collective-permute-done((bf16[128,3584]{1,0:T(8,128)(2,1)S(1)}, bf16[128,3584]{1,0:T(8,128)(2,1)S(1)}, u32[]{:S(2)}, u32[]{:S(2)}) %collective-permute-start.35) | collective-permute-done | bytes 917536 | tf_op jit(solution)/shard_map/ppermute | solution.py:29
  233.8 14.4 %collective-permute-done.44.rest_1_ = bf16[128,3584]{1,0:T(8,128)(2,1)S(1)} collective-permute-done((bf16[128,3584]{1,0:T(8,128)(2,1)S(1)}, bf16[128,3584]{1,0:T(8,128)(2,1)S(1)}, u32[]{:S(2)}, u32[]{:S(2)}) %collective-permute-start.44) | collective-permute-done | bytes 917536 | tf_op jit(solution)/shard_map/ppermute | solution.py:29
  248.4 16.2 %collective-permute-start.47 = (bf16[128,3584]{1,0:T(8,128)(2,1)S(1)}, bf16[128,3584]{1,0:T(8,128)(2,1)S(1)}, u32[]{:S(2)}, u32[]{:S(2)}) collective-permute-start(bf16[128,3584]{1,0:T(8,128)(2,1)S(1)} %shard_map.91.refs_4_), channel_id=1, source_target_pairs={{0,2},{2,0},{4,6},{6,4},{1,3},{3,1},{5,7},{7,5},{8,10},{10,8},{12,... | collective-permute-start | bytes 2752520 | tf_op jit(solution)/shard_map/ppermute | solution.py:29
  268.9 15.0 %collective-permute-done.47 = bf16[128,3584]{1,0:T(8,128)(2,1)S(1)} collective-permute-done((bf16[128,3584]{1,0:T(8,128)(2,1)S(1)}, bf16[128,3584]{1,0:T(8,128)(2,1)S(1)}, u32[]{:S(2)}, u32[]{:S(2)}) %collective-permute-start.47) | collective-permute-done | bytes 917536 | tf_op jit(solution)/shard_map/ppermute | solution.py:29
  (151 shorter events, 67.1 us)
Async XLA Ops:
  6.1 28.1 %collective-permute-start.6 = (bf16[144,3584]{1,0:T(8,128)(2,1)}, bf16[144,3584]{1,0:T(8,128)(2,1)S(1)}, u32[]{:S(2)}, u32[]{:S(2)}) collective-permute-start(bf16[144,3584]{1,0:T(8,128)(2,1)} %pad_maximum_fusion), channel_id=1, source_target_pairs={{2,0},{4,2},{6,4},{3,1},{5,3},{7,5},{10,8},{12,10},{14,12},{11,9},... | collective-permute-start | bytes 3096584 | tf_op jit(solution)/shard_map/ppermute | solution.py:384
  7.4 28.1 %collective-permute-start.5 = (bf16[144,3584]{1,0:T(8,128)(2,1)}, bf16[144,3584]{1,0:T(8,128)(2,1)S(1)}, u32[]{:S(2)}, u32[]{:S(2)}) collective-permute-start(bf16[144,3584]{1,0:T(8,128)(2,1)} %pad_maximum_fusion), channel_id=1, source_target_pairs={{0,2},{2,4},{4,6},{1,3},{3,5},{5,7},{8,10},{10,12},{12,14},{9,11},... | collective-permute-start | bytes 3096584 | tf_op jit(solution)/shard_map/ppermute | solution.py:384
  20.1 24.7 %collective-permute-start.4 = (bf16[80,3584]{1,0:T(8,128)(2,1)S(1)}, bf16[80,3584]{1,0:T(8,128)(2,1)S(1)}, u32[]{:S(2)}, u32[]{:S(2)}) collective-permute-start(bf16[80,3584]{1,0:T(8,128)(2,1)S(1)} %get-tuple-element.74), channel_id=1, source_target_pairs={{0,17},{1,16},{8,25},{9,24},{16,1},{17,0},{24,9},{25,8},{2,19},{3,... | collective-permute-start | bytes 1720328 | tf_op jit(solution)/shard_map/ppermute | solution.py:41
  46.1 24.9 %collective-permute-start.9 = (bf16[144,3584]{1,0:T(8,128)(2,1)S(1)}, bf16[144,3584]{1,0:T(8,128)(2,1)S(1)}, u32[]{:S(2)}, u32[]{:S(2)}) collective-permute-start(bf16[144,3584]{1,0:T(8,128)(2,1)S(1)} %get-tuple-element.82.refs_0_), channel_id=1, source_target_pairs={{2,4},{4,6},{3,5},{5,7},{10,12},{12,14},{11,13},{13,15},{18,20},{2... | collective-permute-start | bytes 3096584 | tf_op jit(solution)/shard_map/ppermute | solution.py:384
  46.9 29.2 %collective-permute-start.10 = (bf16[144,3584]{1,0:T(8,128)(2,1)S(1)}, bf16[144,3584]{1,0:T(8,128)(2,1)S(1)}, u32[]{:S(2)}, u32[]{:S(2)}) collective-permute-start(bf16[144,3584]{1,0:T(8,128)(2,1)S(1)} %get-tuple-element.83.refs_1_), channel_id=1, source_target_pairs={{2,0},{4,2},{3,1},{5,3},{10,8},{12,10},{11,9},{13,11},{18,16},{20,... | collective-permute-start | bytes 3096584 | tf_op jit(solution)/shard_map/ppermute | solution.py:384
  50.2 25.8 %collective-permute-start.11 = (bf16[80,3584]{1,0:T(8,128)(2,1)S(1)}, bf16[80,3584]{1,0:T(8,128)(2,1)S(1)}, u32[]{:S(2)}, u32[]{:S(2)}) collective-permute-start(bf16[80,3584]{1,0:T(8,128)(2,1)S(1)} %get-tuple-element.85), channel_id=1, source_target_pairs={{0,16},{1,17},{8,24},{9,25},{16,0},{17,1},{24,8},{25,9},{2,18},{3,... | collective-permute-start | bytes 1720328 | tf_op jit(solution)/shard_map/ppermute | solution.py:41
  53.5 25.3 %collective-permute-start.13 = (bf16[80,3584]{1,0:T(8,128)(2,1)S(1)}, bf16[80,3584]{1,0:T(8,128)(2,1)S(1)}, u32[]{:S(2)}, u32[]{:S(2)}) collective-permute-start(bf16[80,3584]{1,0:T(8,128)(2,1)S(1)} %get-tuple-element.87), channel_id=1, source_target_pairs={{0,17},{1,16},{8,25},{9,24},{16,1},{17,0},{24,9},{25,8},{2,19},{3,... | collective-permute-start | bytes 1720328 | tf_op jit(solution)/shard_map/ppermute | solution.py:41
  80.1 29.0 %collective-permute-start.14 = (bf16[144,3584]{1,0:T(8,128)(2,1)S(1)}, bf16[144,3584]{1,0:T(8,128)(2,1)S(1)}, u32[]{:S(2)}, u32[]{:S(2)}) collective-permute-start(bf16[144,3584]{1,0:T(8,128)(2,1)S(1)} %get-tuple-element.88), channel_id=1, source_target_pairs={{2,0},{4,6},{3,1},{5,7},{10,8},{12,14},{11,9},{13,15},{18,16},{20,... | collective-permute-start | bytes 3096584 | tf_op jit(solution)/shard_map/ppermute | solution.py:442
  85.0 24.2 %collective-permute-start.17 = (bf16[80,3584]{1,0:T(8,128)(2,1)}, bf16[80,3584]{1,0:T(8,128)(2,1)S(1)}, u32[]{:S(2)}, u32[]{:S(2)}) collective-permute-start(bf16[80,3584]{1,0:T(8,128)(2,1)} %get-tuple-element.94), channel_id=1, source_target_pairs={{0,16},{1,17},{8,24},{9,25},{16,0},{17,1},{24,8},{25,9},{2,18},{3,... | collective-permute-start | bytes 1720328 | tf_op jit(solution)/shard_map/ppermute | solution.py:41
  88.2 25.5 %collective-permute-start.19 = (bf16[80,3584]{1,0:T(8,128)(2,1)S(1)}, bf16[80,3584]{1,0:T(8,128)(2,1)S(1)}, u32[]{:S(2)}, u32[]{:S(2)}) collective-permute-start(bf16[80,3584]{1,0:T(8,128)(2,1)S(1)} %get-tuple-element.96), channel_id=1, source_target_pairs={{0,17},{1,16},{8,25},{9,24},{16,1},{17,0},{24,9},{25,8},{2,19},{3,... | collective-permute-start | bytes 1720328 | tf_op jit(solution)/shard_map/ppermute | solution.py:41
  119.2 24.7 %collective-permute-start.22 = (bf16[80,3584]{1,0:T(8,128)(2,1)S(1)}, bf16[80,3584]{1,0:T(8,128)(2,1)S(1)}, u32[]{:S(2)}, u32[]{:S(2)}) collective-permute-start(bf16[80,3584]{1,0:T(8,128)(2,1)S(1)} %get-tuple-element.101), channel_id=1, source_target_pairs={{0,16},{1,17},{8,24},{9,25},{16,0},{17,1},{24,8},{25,9},{2,18},{3,... | collective-permute-start | bytes 1720328 | tf_op jit(solution)/shard_map/ppermute | solution.py:41
  122.4 26.6 %collective-permute-start.24 = (bf16[80,3584]{1,0:T(8,128)(2,1)S(1)}, bf16[80,3584]{1,0:T(8,128)(2,1)}, u32[]{:S(2)}, u32[]{:S(2)}) collective-permute-start(bf16[80,3584]{1,0:T(8,128)(2,1)S(1)} %get-tuple-element.103), channel_id=1, source_target_pairs={{0,17},{1,16},{8,25},{9,24},{16,1},{17,0},{24,9},{25,8},{2,19},{3,... | collective-permute-start | bytes 1720328 | tf_op jit(solution)/shard_map/ppermute | solution.py:41
  140.7 28.7 %collective-permute-start.28 = (bf16[80,3584]{1,0:T(8,128)(2,1)S(1)}, bf16[80,3584]{1,0:T(8,128)(2,1)S(1)}, u32[]{:S(2)}, u32[]{:S(2)}) collective-permute-start(bf16[80,3584]{1,0:T(8,128)(2,1)S(1)} %get-tuple-element.112), channel_id=1, source_target_pairs={{0,16},{1,17},{8,24},{9,25},{16,0},{17,1},{24,8},{25,9},{2,18},{3,... | collective-permute-start | bytes 1720328 | tf_op jit(solution)/shard_map/ppermute | solution.py:41
  142.4 27.4 %collective-permute-start.29 = (bf16[80,3584]{1,0:T(8,128)(2,1)S(1)}, bf16[80,3584]{1,0:T(8,128)(2,1)S(1)}, u32[]{:S(2)}, u32[]{:S(2)}) collective-permute-start(bf16[80,3584]{1,0:T(8,128)(2,1)S(1)} %get-tuple-element.113), channel_id=1, source_target_pairs={{0,1},{1,0},{8,9},{9,8},{16,17},{17,16},{24,25},{25,24},{2,3},{3,2... | collective-permute-start | bytes 1720328 | tf_op jit(solution)/shard_map/ppermute | solution.py:41
  143.9 29.6 %collective-permute-start.30 = (bf16[80,3584]{1,0:T(8,128)(2,1)}, bf16[80,3584]{1,0:T(8,128)(2,1)S(1)}, u32[]{:S(2)}, u32[]{:S(2)}) collective-permute-start(bf16[80,3584]{1,0:T(8,128)(2,1)} %get-tuple-element.114), channel_id=1, source_target_pairs={{0,17},{1,16},{8,25},{9,24},{16,1},{17,0},{24,9},{25,8},{2,19},{3,... | collective-permute-start | bytes 1720328 | tf_op jit(solution)/shard_map/ppermute | solution.py:41
  169.4 27.5 %collective-permute-start.27 = (bf16[80,3584]{1,0:T(8,128)(2,1)}, bf16[80,3584]{1,0:T(8,128)(2,1)S(1)}, u32[]{:S(2)}, u32[]{:S(2)}) collective-permute-start(bf16[80,3584]{1,0:T(8,128)(2,1)} %get-tuple-element.108), channel_id=1, source_target_pairs={{0,17},{1,16},{8,25},{9,24},{16,1},{17,0},{24,9},{25,8},{2,19},{3,... | collective-permute-start | bytes 1720328 | tf_op jit(solution)/shard_map/ppermute | solution.py:41
  177.9 46.4 %collective-permute-start.35 = (bf16[128,3584]{1,0:T(8,128)(2,1)S(1)}, bf16[128,3584]{1,0:T(8,128)(2,1)S(1)}, u32[]{:S(2)}, u32[]{:S(2)}) collective-permute-start(bf16[128,3584]{1,0:T(8,128)(2,1)S(1)} %shard_map.85.refs_4_), channel_id=1, source_target_pairs={{0,4},{2,6},{4,0},{6,2},{1,5},{3,7},{5,1},{7,3},{8,12},{10,14},{12... | collective-permute-start | bytes 2752520 | tf_op jit(solution)/shard_map/ppermute | solution.py:29
  199.2 26.9 %collective-permute-start.39 = (bf16[80,3584]{1,0:T(8,128)(2,1)S(1)}, bf16[80,3584]{1,0:T(8,128)(2,1)S(1)}, u32[]{:S(2)}, u32[]{:S(2)}) collective-permute-start(bf16[80,3584]{1,0:T(8,128)(2,1)S(1)} %get-tuple-element.126), channel_id=1, source_target_pairs={{0,16},{1,17},{8,24},{9,25},{16,0},{17,1},{24,8},{25,9},{2,18},{3,... | collective-permute-start | bytes 1720328 | tf_op jit(solution)/shard_map/ppermute | solution.py:41
  200.9 25.3 %collective-permute-start.40 = (bf16[80,3584]{1,0:T(8,128)(2,1)S(1)}, bf16[80,3584]{1,0:T(8,128)(2,1)S(1)}, u32[]{:S(2)}, u32[]{:S(2)}) collective-permute-start(bf16[80,3584]{1,0:T(8,128)(2,1)S(1)} %get-tuple-element.127), channel_id=1, source_target_pairs={{0,1},{1,0},{8,9},{9,8},{16,17},{17,16},{24,25},{25,24},{2,3},{3,2... | collective-permute-start | bytes 1720328 | tf_op jit(solution)/shard_map/ppermute | solution.py:41
  202.4 25.3 %collective-permute-start.41 = (bf16[80,3584]{1,0:T(8,128)(2,1)S(1)}, bf16[80,3584]{1,0:T(8,128)(2,1)S(1)}, u32[]{:S(2)}, u32[]{:S(2)}) collective-permute-start(bf16[80,3584]{1,0:T(8,128)(2,1)S(1)} %get-tuple-element.128), channel_id=1, source_target_pairs={{0,17},{1,16},{8,25},{9,24},{16,1},{17,0},{24,9},{25,8},{2,19},{3,... | collective-permute-start | bytes 1720328 | tf_op jit(solution)/shard_map/ppermute | solution.py:41
  229.9 34.7 %collective-permute-start.36 = (bf16[80,3584]{1,0:T(8,128)(2,1)S(1)}, bf16[80,3584]{1,0:T(8,128)(2,1)S(1)}, u32[]{:S(2)}, u32[]{:S(2)}) collective-permute-start(bf16[80,3584]{1,0:T(8,128)(2,1)S(1)} %get-tuple-element.123), channel_id=1, source_target_pairs={{0,16},{1,17},{8,24},{9,25},{16,0},{17,1},{24,8},{25,9},{2,18},{3,... | collective-permute-start | bytes 1720328 | tf_op jit(solution)/shard_map/ppermute | solution.py:41
  231.6 33.0 %collective-permute-start.37 = (bf16[80,3584]{1,0:T(8,128)(2,1)S(1)}, bf16[80,3584]{1,0:T(8,128)(2,1)S(1)}, u32[]{:S(2)}, u32[]{:S(2)}) collective-permute-start(bf16[80,3584]{1,0:T(8,128)(2,1)S(1)} %get-tuple-element.124), channel_id=1, source_target_pairs={{0,1},{1,0},{8,9},{9,8},{16,17},{17,16},{24,25},{25,24},{2,3},{3,2... | collective-permute-start | bytes 1720328 | tf_op jit(solution)/shard_map/ppermute | solution.py:41
  233.1 31.5 %collective-permute-start.38 = (bf16[80,3584]{1,0:T(8,128)(2,1)S(1)}, bf16[80,3584]{1,0:T(8,128)(2,1)S(1)}, u32[]{:S(2)}, u32[]{:S(2)}) collective-permute-start(bf16[80,3584]{1,0:T(8,128)(2,1)S(1)} %get-tuple-element.125), channel_id=1, source_target_pairs={{0,17},{1,16},{8,25},{9,24},{16,1},{17,0},{24,9},{25,8},{2,19},{3,... | collective-permute-start | bytes 1720328 | tf_op jit(solution)/shard_map/ppermute | solution.py:41
  248.4 35.5 %collective-permute-start.47 = (bf16[128,3584]{1,0:T(8,128)(2,1)S(1)}, bf16[128,3584]{1,0:T(8,128)(2,1)S(1)}, u32[]{:S(2)}, u32[]{:S(2)}) collective-permute-start(bf16[128,3584]{1,0:T(8,128)(2,1)S(1)} %shard_map.91.refs_4_), channel_id=1, source_target_pairs={{0,2},{2,0},{4,6},{6,4},{1,3},{3,1},{5,7},{7,5},{8,10},{10,8},{12,... | collective-permute-start | bytes 2752520 | tf_op jit(solution)/shard_map/ppermute | solution.py:29
  (44 other events, 414.7 us)

commit v2 on v1

--- a/solution.py
+++ b/solution.py
@@ -59,7 +59,7 @@
         out_specs=out_specs,
         out_shape=out_shape,
         scratch_shapes=scratch,
-        cost_estimate=pl.CostEstimate(flops=flops, bytes_accessed=nbytes, transcendentals=0),
+        cost_estimate=pl.CostEstimate(flops=1, bytes_accessed=1, transcendentals=0),
         compiler_params=pltpu.CompilerParams(
             dimension_semantics=("arbitrary",), vmem_limit_bytes=limit
         ),
@@ -303,13 +303,16 @@
 
 def add_kernel(n_after, own_ref, left_ref, right_ref, *rest):
     out_ref = rest[n_after]
-    half = left_ref.shape[1]
+    tok, half = left_ref.shape
     for at, ref in enumerate((left_ref, right_ref)):
         part = own_ref[:, at * half : (at + 1) * half] + ref[...].astype(jnp.float32)
-        out_ref[:, at * half : (at + 1) * half] = part.astype(out_ref.dtype)
-
-
-def added(own, sib, after):
+        out_ref[:tok, at * half : (at + 1) * half] = part.astype(out_ref.dtype)
+    if out_ref.shape[0] > tok:
+        rest_of = out_ref.shape[0] - tok
+        out_ref[tok:, :] = jnp.zeros((rest_of, 2 * half), out_ref.dtype)
+
+
+def added(own, sib, after, extra=0):
     tok, width = own.shape
     half = pl.BlockSpec((tok, width // 2), lambda j: (0, 0))
     whole = pl.BlockSpec((tok, width), lambda j: (0, 0))
@@ -317,8 +320,8 @@
         functools.partial(add_kernel, len(after)),
         (1,),
         [whole, half, half],
-        whole,
-        jax.ShapeDtypeStruct((tok, width), jnp.bfloat16),
+        pl.BlockSpec((tok + extra, width), lambda j: (0, 0)),
+        jax.ShapeDtypeStruct((tok + extra, width), jnp.bfloat16),
         [],
         tok * width,
         8 * tok * width,
@@ -399,6 +402,15 @@
             for part, (dx, dy) in zip(values, rel)
         ]
 
+    def send_free(dz):
+        own, sib = halves[dz]
+        part = own + jnp.concatenate(sib, axis=1).astype(jnp.float32)
+        sums[dz] = swap(part.astype(jnp.bfloat16), "plane", dz)
+
+    def tick(*after):
+        (out,) = passed([meta[:, : 3 * tok_rows]], last + list(after))
+        last[:] = [out]
+
     def dispatch(dz, *after):
         sent, weights[dz] = select(
             want, tokens[dz], siblings[dz], top_k, parts, last + list(after)
@@ -417,13 +429,17 @@
             last[:] = [sent[0]]
         halves[dz] = in_plane(sent)
 
-    def collect(dz, *after):
+    def collect(dz, *after, whole=False):
         own, *sib = combine(weights[dz], halves[dz], last + list(after))
         last[:] = [sib[0]]
+        if whole:
+            came = swap(jnp.concatenate(sib, axis=1), "core", 1)
+            halves[dz] = own, [came[:, :middle], came[:, middle:]]
+            return
         halves[dz] = own, [swap(half, "core", 1) for half in sib]
 
-    def send_home(dz, *after):
-        part = added(*halves[dz], last + list(after))
+    def send_home(dz, *after, extra=0):
+        part = added(*halves[dz], last + list(after), extra)
         last[:] = [part]
         sums[dz] = swap(part, "plane", dz)
 
@@ -448,9 +464,8 @@
         [up1, down1, ends],
         0,
         0,
-        *arrived[2],
-    )
-    dispatch(3)
+    )
+    dispatch(3, *arrived[2])
     apply(2)
     give_back(2)
     apply(3)
@@ -458,17 +473,19 @@
     collect(2)
     send_home(2)
     give_back(1, late=True)
-    collect(3)
-    send_home(3, sums[2])
+    collect(3, whole=True)
+    tick(sums[2])
+    send_home(3)
     give_back(0, late=True)
     collect(1)
-    send_home(1, sums[3])
+    send_free(1)
+    tick(sums[3])
     collect(0)
     own, sib = halves[0]
     sums[0] = own + jnp.concatenate(sib, axis=1).astype(jnp.float32)
     total = sums[0]
     for dz in range(1, zs):
-        total = total + sums[dz].astype(jnp.float32)
+        total = total + sums[dz][:tok_rows].astype(jnp.float32)
     return total.astype(jnp.bfloat16)
 
 

time: 286 us -> 276 us (0.965)
  starting transfers between devices: 67.2 us -> 55.4 us
  waiting for transfers between devices: 120 us -> 117 us
    ppermute x19 -> x18, starting transfers between devices: 27.9 us -> 16.9 us  [swap(): return lax.ppermute(value, axis, [(i, i ^ delta) for i in range(size)])]
    ppermute x24, waiting for transfers between devices: 38.9 us -> 43 us  [swap_in_plane(): return lax.ppermute(value, PLANE, pairs)]
    ppermute x19 -> x18, waiting for transfers between devices: 57.4 us -> 53.8 us  [swap(): return lax.ppermute(value, axis, [(i, i ^ delta) for i in range(size)])]
    ppermute x1, waiting for transfers between devices: 3.43 us -> 0.01 us  [shards(): ends = lax.ppermute(second, 'plane', [(1, 0), (2, 3)])]
    pallas_call x20 -> x21, Pallas kernels: 88.8 us -> 89.5 us  [call(): pl.pallas_call(kernel, grid=grid, in_specs=list(in_specs) + [pl.BlockSpec...]
  transfers between devices with their start and end apart: 48 -> 47, of which waited for: 24 -> 21; matrix products, arithmetic and copies ran while one was open for 0% -> 1% of each run, Pallas kernels for 30% -> 31%
where the time goes in v2:
time: 276 us; the launch traced here: 273 us
  waiting for transfers between devices  117 us (42%)
  Pallas kernels  89.5 us (32%)
  starting transfers between devices  55.4 us (20%)
  local copies, waits for them, and re-layouts  5.17 us (2%)
  other arithmetic  5.07 us (2%)
    pallas_call x21, Pallas kernels, call(): pl.pallas_call(kernel, grid=grid, in_specs=list(in_specs) + [pl.BlockSpec...  89.5 us
    ppermute x18, waiting for transfers between devices, swap(): return lax.ppermute(value, axis, [(i, i ^ delta) for i in range(size)])  53.8 us
    ppermute x24, waiting for transfers between devices, swap_in_plane(): return lax.ppermute(value, PLANE, pairs)  43 us
    ppermute x24, starting transfers between devices, swap_in_plane(): return lax.ppermute(value, PLANE, pairs)  28.2 us
    ppermute x4, waiting for transfers between devices, hop(): return lax.ppermute(value, 'plane', [(z, z + step) for z in sources])  20.3 us
    ppermute x18, starting transfers between devices, swap(): return lax.ppermute(value, axis, [(i, i ^ delta) for i in range(size)])  16.9 us
    ppermute x4, starting transfers between devices, hop(): return lax.ppermute(value, 'plane', [(z, z + step) for z in sources])  8.91 us
  transfers between devices with their start and end apart: 47, of which 21 were waited for; matrix products, arithmetic and copies ran while one was open for 1% of the time, Pallas kernels for 31%

profile of v2, /device:TPU:0, one launch (start us, length us, event | category | flops | bytes accessed | tf_op | source)
XLA Modules:
  0.0 272.9 jit_solution(10121842560483411370)
XLA Ops:
  7.4 5.6 %collective-permute-start.5 = (bf16[144,3584]{1,0:T(8,128)(2,1)}, bf16[144,3584]{1,0:T(8,128)(2,1)S(1)}, u32[]{:S(2)}, u32[]{:S(2)}) collective-permute-start(bf16[144,3584]{1,0:T(8,128)(2,1)} %pad_maximum_fusion), channel_id=1, source_target_pairs={{0,2},{2,4},{4,6},{1,3},{3,5},{5,7},{8,10},{10,12},{12,14},{9,11},... | collective-permute-start | bytes 3096584 | tf_op jit(solution)/shard_map/ppermute | solution.py:387
  13.4 3.2 %shard_map.73 = (bf16[80,3584]{1,0:T(8,128)(2,1)S(1)}, bf16[80,3584]{1,0:T(8,128)(2,1)S(1)}, bf16[80,3584]{1,0:T(8,128)(2,1)S(1)}, bf16[80,3584]{1,0:T(8,128)(2,1)S(1)}, bf16[256,320]{1,0:T(8,128)(2,1)S(1)}) custom-call(f32[320,1]{1,0:T(8,128)S(1)} %add.114.want_ref, bf16[144,1792]{1,0:T(8,128)(2,1)S(1)} %pad_maximum_fusion.2.refs_0_, ...), custom_call_target="tpu_custom_call" | custom-call | flops 1 | bytes 1 | tf_op jit(solution)/shard_map/pallas_call | solution.py:55
  16.6 2.0 collective-permute-start.2
  20.2 14.0 %collective-permute-done.6.refs_1_ = bf16[144,3584]{1,0:T(8,128)(2,1)S(1)} collective-permute-done((bf16[144,3584]{1,0:T(8,128)(2,1)}, bf16[144,3584]{1,0:T(8,128)(2,1)S(1)}, u32[]{:S(2)}, u32[]{:S(2)}) %collective-permute-start.6) | collective-permute-done | bytes 1032224 | tf_op jit(solution)/shard_map/ppermute | solution.py:387
  35.5 9.3 %collective-permute-done.4.refs_6_.refs_3_ = bf16[80,3584]{1,0:T(8,128)(2,1)S(1)} collective-permute-done((bf16[80,3584]{1,0:T(8,128)(2,1)S(1)}, bf16[80,3584]{1,0:T(8,128)(2,1)S(1)}, u32[]{:S(2)}, u32[]{:S(2)}) %collective-permute-start.4) | collective-permute-done | bytes 573472 | tf_op jit(solution)/shard_map/ppermute | solution.py:41
  48.3 2.0 shard_map.75
  53.8 17.2 %shard_map.76 = (bf16[80,3584]{1,0:T(8,128)(2,1)S(1)}, bf16[80,3584]{1,0:T(8,128)(2,1)S(1)}, bf16[80,3584]{1,0:T(8,128)(2,1)S(1)}, bf16[80,3584]{1,0:T(8,128)(2,1)}) custom-call(bf16[80,3584]{1,0:T(8,128)(2,1)} %copy-done.1, bf16[80,3584]{1,0:T(8,128)(2,1)} %copy-done.4, bf16[80,3584]{1,0:T(8,128)(2,1)} %copy-done.7, bf16[80,3584]{1,0:T(8,128)(2,1)} %copy-done.10, ...), custom_call_target="tpu_custom_call" | custom-call | flops 1 | bytes 1 | tf_op jit(solution)/shard_map/pallas_call | solution.py:55
  71.1 5.0 %collective-permute-done.10.refs_1_ = bf16[144,3584]{1,0:T(8,128)(2,1)S(1)} collective-permute-done((bf16[144,3584]{1,0:T(8,128)(2,1)S(1)}, bf16[144,3584]{1,0:T(8,128)(2,1)S(1)}, u32[]{:S(2)}, u32[]{:S(2)}) %collective-permute-start.10) | collective-permute-done | bytes 1032224 | tf_op jit(solution)/shard_map/ppermute | solution.py:387
  76.1 2.7 %collective-permute-done.13.refs_6_.refs_3_ = bf16[80,3584]{1,0:T(8,128)(2,1)S(1)} collective-permute-done((bf16[80,3584]{1,0:T(8,128)(2,1)S(1)}, bf16[80,3584]{1,0:T(8,128)(2,1)S(1)}, u32[]{:S(2)}, u32[]{:S(2)}) %collective-permute-start.13) | collective-permute-done | bytes 573472 | tf_op jit(solution)/shard_map/ppermute | solution.py:41
  83.8 2.7 shard_map.78
  90.0 17.2 %shard_map.79 = (bf16[80,3584]{1,0:T(8,128)(2,1)S(1)}, bf16[80,3584]{1,0:T(8,128)(2,1)S(1)}, bf16[80,3584]{1,0:T(8,128)(2,1)S(1)}, bf16[80,3584]{1,0:T(8,128)(2,1)}) custom-call(bf16[80,3584]{1,0:T(8,128)(2,1)} %copy-done, bf16[80,3584]{1,0:T(8,128)(2,1)} %copy-done.3, bf16[80,3584]{1,0:T(8,128)(2,1)} %copy-done.5, bf16[80,3584]{1,0:T(8,128)(2,1)} %copy-done.8, ...), custom_call_target="tpu_custom_call" | custom-call | flops 1 | bytes 1 | tf_op jit(solution)/shard_map/pallas_call | solution.py:55
  108.3 6.9 %collective-permute-done.21.refs_8_.refs_3_ = bf16[80,3584]{1,0:T(8,128)(2,1)S(1)} collective-permute-done((bf16[80,3584]{1,0:T(8,128)(2,1)S(1)}, bf16[80,3584]{1,0:T(8,128)(2,1)S(1)}, u32[]{:S(2)}, u32[]{:S(2)}) %collective-permute-start.21) | collective-permute-done | bytes 573472 | tf_op jit(solution)/shard_map/ppermute | solution.py:41
  115.3 2.6 shard_map.81
  121.5 17.2 %shard_map.82 = (bf16[80,3584]{1,0:T(8,128)(2,1)S(1)}, bf16[80,3584]{1,0:T(8,128)(2,1)S(1)}, bf16[80,3584]{1,0:T(8,128)(2,1)S(1)}, bf16[80,3584]{1,0:T(8,128)(2,1)}) custom-call(bf16[80,3584]{1,0:T(8,128)(2,1)} %copy-done.2, bf16[80,3584]{1,0:T(8,128)(2,1)} %copy-done.6, bf16[80,3584]{1,0:T(8,128)(2,1)} %copy-done.9, bf16[80,3584]{1,0:T(8,128)(2,1)} %copy-done.11, ...), custom_call_target="tpu_custom_call" | custom-call | flops 1 | bytes 1 | tf_op jit(solution)/shard_map/pallas_call | solution.py:55
  143.0 4.7 %collective-permute-done.24.refs_3_ = bf16[80,3584]{1,0:T(8,128)(2,1)S(1)} collective-permute-done((bf16[80,3584]{1,0:T(8,128)(2,1)S(1)}, bf16[80,3584]{1,0:T(8,128)(2,1)S(1)}, u32[]{:S(2)}, u32[]{:S(2)}) %collective-permute-start.24) | collective-permute-done | bytes 573472 | tf_op jit(solution)/shard_map/ppermute | solution.py:41
  148.5 17.3 %shard_map.83 = (bf16[80,3584]{1,0:T(8,128)(2,1)S(1)}, bf16[80,3584]{1,0:T(8,128)(2,1)S(1)}, bf16[80,3584]{1,0:T(8,128)(2,1)S(1)}, bf16[80,3584]{1,0:T(8,128)(2,1)}) custom-call(bf16[80,3584]{1,0:T(8,128)(2,1)} %copy-done.16, bf16[80,3584]{1,0:T(8,128)(2,1)} %copy-done.18, bf16[80,3584]{1,0:T(8,128)(2,1)} %copy-done.19, bf16[80,3584]{1,0:T(8,128)(2,1)} %copy-done.20, ...), custom_call_target="tpu_custom_call" | custom-call | flops 1 | bytes 1 | tf_op jit(solution)/shard_map/pallas_call | solution.py:55
  169.3 3.0 %collective-permute-done.30.refs_3_ = bf16[80,3584]{1,0:T(8,128)(2,1)S(1)} collective-permute-done((bf16[80,3584]{1,0:T(8,128)(2,1)}, bf16[80,3584]{1,0:T(8,128)(2,1)S(1)}, u32[]{:S(2)}, u32[]{:S(2)}) %collective-permute-start.30) | collective-permute-done | bytes 573472 | tf_op jit(solution)/shard_map/ppermute | solution.py:41
  176.7 6.1 %collective-permute-start.34 = (bf16[128,3584]{1,0:T(8,128)(2,1)S(1)}, bf16[128,3584]{1,0:T(8,128)(2,1)S(1)}, u32[]{:S(2)}, u32[]{:S(2)}) collective-permute-start(bf16[128,3584]{1,0:T(8,128)(2,1)S(1)} %shard_map.85.refs_4_), channel_id=1, source_target_pairs={{0,4},{2,6},{4,0},{6,2},{1,5},{3,7},{5,1},{7,3},{8,12},{10,14},{12... | collective-permute-start | bytes 2752520 | tf_op jit(solution)/shard_map/ppermute | solution.py:29
  184.8 9.8 %collective-permute-done.27.refs_3_ = bf16[80,3584]{1,0:T(8,128)(2,1)S(1)} collective-permute-done((bf16[80,3584]{1,0:T(8,128)(2,1)}, bf16[80,3584]{1,0:T(8,128)(2,1)S(1)}, u32[]{:S(2)}, u32[]{:S(2)}) %collective-permute-start.27) | collective-permute-done | bytes 573472 | tf_op jit(solution)/shard_map/ppermute | solution.py:41
  200.0 23.2 %collective-permute-done.34.refs_2_ = bf16[128,3584]{1,0:T(8,128)(2,1)S(1)} collective-permute-done((bf16[128,3584]{1,0:T(8,128)(2,1)S(1)}, bf16[128,3584]{1,0:T(8,128)(2,1)S(1)}, u32[]{:S(2)}, u32[]{:S(2)}) %collective-permute-start.34) | collective-permute-done | bytes 917536 | tf_op jit(solution)/shard_map/ppermute | solution.py:29
  233.0 4.9 %collective-permute-start.46 = (bf16[128,3584]{1,0:T(8,128)(2,1)S(1)}, bf16[128,3584]{1,0:T(8,128)(2,1)S(1)}, u32[]{:S(2)}, u32[]{:S(2)}) collective-permute-start(bf16[128,3584]{1,0:T(8,128)(2,1)S(1)} %add_convert_fusion.1), channel_id=1, source_target_pairs={{0,2},{2,0},{4,6},{6,4},{1,3},{3,1},{5,7},{7,5},{8,10},{10,8},{12,... | collective-permute-start | bytes 2752520 | tf_op jit(solution)/shard_map/ppermute | solution.py:29
  237.9 14.8 %collective-permute-done.41.refs_2_ = bf16[128,3584]{1,0:T(8,128)(2,1)S(1)} collective-permute-done((bf16[128,3584]{1,0:T(8,128)(2,1)S(1)}, bf16[128,3584]{1,0:T(8,128)(2,1)S(1)}, u32[]{:S(2)}, u32[]{:S(2)}) %collective-permute-start.41) | collective-permute-done | bytes 917536 | tf_op jit(solution)/shard_map/ppermute | solution.py:29
  252.7 4.8 %collective-permute-done.37.refs_3_ = bf16[80,3584]{1,0:T(8,128)(2,1)S(1)} collective-permute-done((bf16[80,3584]{1,0:T(8,128)(2,1)S(1)}, bf16[80,3584]{1,0:T(8,128)(2,1)S(1)}, u32[]{:S(2)}, u32[]{:S(2)}) %collective-permute-start.37) | collective-permute-done | bytes 573472 | tf_op jit(solution)/shard_map/ppermute | solution.py:41
  259.8 11.7 %collective-permute-done.46 = bf16[128,3584]{1,0:T(8,128)(2,1)S(1)} collective-permute-done((bf16[128,3584]{1,0:T(8,128)(2,1)S(1)}, bf16[128,3584]{1,0:T(8,128)(2,1)S(1)}, u32[]{:S(2)}, u32[]{:S(2)}) %collective-permute-start.46) | collective-permute-done | bytes 917536 | tf_op jit(solution)/shard_map/ppermute | solution.py:29
  (155 shorter events, 64.5 us)
Async XLA Ops:
  6.1 28.1 %collective-permute-start.6 = (bf16[144,3584]{1,0:T(8,128)(2,1)}, bf16[144,3584]{1,0:T(8,128)(2,1)S(1)}, u32[]{:S(2)}, u32[]{:S(2)}) collective-permute-start(bf16[144,3584]{1,0:T(8,128)(2,1)} %pad_maximum_fusion), channel_id=1, source_target_pairs={{2,0},{4,2},{6,4},{3,1},{5,3},{7,5},{10,8},{12,10},{14,12},{11,9},... | collective-permute-start | bytes 3096584 | tf_op jit(solution)/shard_map/ppermute | solution.py:387
  7.4 28.1 %collective-permute-start.5 = (bf16[144,3584]{1,0:T(8,128)(2,1)}, bf16[144,3584]{1,0:T(8,128)(2,1)S(1)}, u32[]{:S(2)}, u32[]{:S(2)}) collective-permute-start(bf16[144,3584]{1,0:T(8,128)(2,1)} %pad_maximum_fusion), channel_id=1, source_target_pairs={{0,2},{2,4},{4,6},{1,3},{3,5},{5,7},{8,10},{10,12},{12,14},{9,11},... | collective-permute-start | bytes 3096584 | tf_op jit(solution)/shard_map/ppermute | solution.py:387
  20.1 24.7 %collective-permute-start.4 = (bf16[80,3584]{1,0:T(8,128)(2,1)S(1)}, bf16[80,3584]{1,0:T(8,128)(2,1)S(1)}, u32[]{:S(2)}, u32[]{:S(2)}) collective-permute-start(bf16[80,3584]{1,0:T(8,128)(2,1)S(1)} %get-tuple-element.74), channel_id=1, source_target_pairs={{0,17},{1,16},{8,25},{9,24},{16,1},{17,0},{24,9},{25,8},{2,19},{3,... | collective-permute-start | bytes 1720328 | tf_op jit(solution)/shard_map/ppermute | solution.py:41
  46.1 24.9 %collective-permute-start.9 = (bf16[144,3584]{1,0:T(8,128)(2,1)S(1)}, bf16[144,3584]{1,0:T(8,128)(2,1)S(1)}, u32[]{:S(2)}, u32[]{:S(2)}) collective-permute-start(bf16[144,3584]{1,0:T(8,128)(2,1)S(1)} %get-tuple-element.82.refs_0_), channel_id=1, source_target_pairs={{2,4},{4,6},{3,5},{5,7},{10,12},{12,14},{11,13},{13,15},{18,20},{2... | collective-permute-start | bytes 3096584 | tf_op jit(solution)/shard_map/ppermute | solution.py:387
  46.9 29.2 %collective-permute-start.10 = (bf16[144,3584]{1,0:T(8,128)(2,1)S(1)}, bf16[144,3584]{1,0:T(8,128)(2,1)S(1)}, u32[]{:S(2)}, u32[]{:S(2)}) collective-permute-start(bf16[144,3584]{1,0:T(8,128)(2,1)S(1)} %get-tuple-element.83.refs_1_), channel_id=1, source_target_pairs={{2,0},{4,2},{3,1},{5,3},{10,8},{12,10},{11,9},{13,11},{18,16},{20,... | collective-permute-start | bytes 3096584 | tf_op jit(solution)/shard_map/ppermute | solution.py:387
  50.3 25.8 %collective-permute-start.11 = (bf16[80,3584]{1,0:T(8,128)(2,1)S(1)}, bf16[80,3584]{1,0:T(8,128)(2,1)S(1)}, u32[]{:S(2)}, u32[]{:S(2)}) collective-permute-start(bf16[80,3584]{1,0:T(8,128)(2,1)S(1)} %get-tuple-element.85), channel_id=1, source_target_pairs={{0,16},{1,17},{8,24},{9,25},{16,0},{17,1},{24,8},{25,9},{2,18},{3,... | collective-permute-start | bytes 1720328 | tf_op jit(solution)/shard_map/ppermute | solution.py:41
  52.0 24.1 %collective-permute-start.12 = (bf16[80,3584]{1,0:T(8,128)(2,1)S(1)}, bf16[80,3584]{1,0:T(8,128)(2,1)S(1)}, u32[]{:S(2)}, u32[]{:S(2)}) collective-permute-start(bf16[80,3584]{1,0:T(8,128)(2,1)S(1)} %get-tuple-element.86), channel_id=1, source_target_pairs={{0,1},{1,0},{8,9},{9,8},{16,17},{17,16},{24,25},{25,24},{2,3},{3,2... | collective-permute-start | bytes 1720328 | tf_op jit(solution)/shard_map/ppermute | solution.py:41
  53.5 25.3 %collective-permute-start.13 = (bf16[80,3584]{1,0:T(8,128)(2,1)S(1)}, bf16[80,3584]{1,0:T(8,128)(2,1)S(1)}, u32[]{:S(2)}, u32[]{:S(2)}) collective-permute-start(bf16[80,3584]{1,0:T(8,128)(2,1)S(1)} %get-tuple-element.87), channel_id=1, source_target_pairs={{0,17},{1,16},{8,25},{9,24},{16,1},{17,0},{24,9},{25,8},{2,19},{3,... | collective-permute-start | bytes 1720328 | tf_op jit(solution)/shard_map/ppermute | solution.py:41
  79.7 27.6 %collective-permute-start.14 = (bf16[144,3584]{1,0:T(8,128)(2,1)S(1)}, bf16[144,3584]{1,0:T(8,128)(2,1)S(1)}, u32[]{:S(2)}, u32[]{:S(2)}) collective-permute-start(bf16[144,3584]{1,0:T(8,128)(2,1)S(1)} %get-tuple-element.88), channel_id=1, source_target_pairs={{2,0},{4,6},{3,1},{5,7},{10,8},{12,14},{11,9},{13,15},{18,16},{20,... | collective-permute-start | bytes 3096584 | tf_op jit(solution)/shard_map/ppermute | solution.py:458
  89.7 25.6 %collective-permute-start.21 = (bf16[80,3584]{1,0:T(8,128)(2,1)S(1)}, bf16[80,3584]{1,0:T(8,128)(2,1)S(1)}, u32[]{:S(2)}, u32[]{:S(2)}) collective-permute-start(bf16[80,3584]{1,0:T(8,128)(2,1)S(1)} %get-tuple-element.98), channel_id=1, source_target_pairs={{0,17},{1,16},{8,25},{9,24},{16,1},{17,0},{24,9},{25,8},{2,19},{3,... | collective-permute-start | bytes 1720328 | tf_op jit(solution)/shard_map/ppermute | solution.py:41
  117.9 24.8 %collective-permute-start.22 = (bf16[80,3584]{1,0:T(8,128)(2,1)}, bf16[80,3584]{1,0:T(8,128)(2,1)S(1)}, u32[]{:S(2)}, u32[]{:S(2)}) collective-permute-start(bf16[80,3584]{1,0:T(8,128)(2,1)} %get-tuple-element.101), channel_id=1, source_target_pairs={{0,16},{1,17},{8,24},{9,25},{16,0},{17,1},{24,8},{25,9},{2,18},{3,... | collective-permute-start | bytes 1720328 | tf_op jit(solution)/shard_map/ppermute | solution.py:41
  121.1 26.6 %collective-permute-start.24 = (bf16[80,3584]{1,0:T(8,128)(2,1)S(1)}, bf16[80,3584]{1,0:T(8,128)(2,1)S(1)}, u32[]{:S(2)}, u32[]{:S(2)}) collective-permute-start(bf16[80,3584]{1,0:T(8,128)(2,1)S(1)} %get-tuple-element.103), channel_id=1, source_target_pairs={{0,17},{1,16},{8,25},{9,24},{16,1},{17,0},{24,9},{25,8},{2,19},{3,... | collective-permute-start | bytes 1720328 | tf_op jit(solution)/shard_map/ppermute | solution.py:41
  139.5 29.4 %collective-permute-start.28 = (bf16[80,3584]{1,0:T(8,128)(2,1)S(1)}, bf16[80,3584]{1,0:T(8,128)(2,1)S(1)}, u32[]{:S(2)}, u32[]{:S(2)}) collective-permute-start(bf16[80,3584]{1,0:T(8,128)(2,1)S(1)} %get-tuple-element.112), channel_id=1, source_target_pairs={{0,16},{1,17},{8,24},{9,25},{16,0},{17,1},{24,8},{25,9},{2,18},{3,... | collective-permute-start | bytes 1720328 | tf_op jit(solution)/shard_map/ppermute | solution.py:41
  141.2 28.1 %collective-permute-start.29 = (bf16[80,3584]{1,0:T(8,128)(2,1)S(1)}, bf16[80,3584]{1,0:T(8,128)(2,1)S(1)}, u32[]{:S(2)}, u32[]{:S(2)}) collective-permute-start(bf16[80,3584]{1,0:T(8,128)(2,1)S(1)} %get-tuple-element.113), channel_id=1, source_target_pairs={{0,1},{1,0},{8,9},{9,8},{16,17},{17,16},{24,25},{25,24},{2,3},{3,2... | collective-permute-start | bytes 1720328 | tf_op jit(solution)/shard_map/ppermute | solution.py:41
  142.7 29.6 %collective-permute-start.30 = (bf16[80,3584]{1,0:T(8,128)(2,1)}, bf16[80,3584]{1,0:T(8,128)(2,1)S(1)}, u32[]{:S(2)}, u32[]{:S(2)}) collective-permute-start(bf16[80,3584]{1,0:T(8,128)(2,1)} %get-tuple-element.114), channel_id=1, source_target_pairs={{0,17},{1,16},{8,25},{9,24},{16,1},{17,0},{24,9},{25,8},{2,19},{3,... | collective-permute-start | bytes 1720328 | tf_op jit(solution)/shard_map/ppermute | solution.py:41
  169.0 25.6 %collective-permute-start.27 = (bf16[80,3584]{1,0:T(8,128)(2,1)}, bf16[80,3584]{1,0:T(8,128)(2,1)S(1)}, u32[]{:S(2)}, u32[]{:S(2)}) collective-permute-start(bf16[80,3584]{1,0:T(8,128)(2,1)} %get-tuple-element.108), channel_id=1, source_target_pairs={{0,17},{1,16},{8,25},{9,24},{16,1},{17,0},{24,9},{25,8},{2,19},{3,... | collective-permute-start | bytes 1720328 | tf_op jit(solution)/shard_map/ppermute | solution.py:41
  176.7 46.4 %collective-permute-start.34 = (bf16[128,3584]{1,0:T(8,128)(2,1)S(1)}, bf16[128,3584]{1,0:T(8,128)(2,1)S(1)}, u32[]{:S(2)}, u32[]{:S(2)}) collective-permute-start(bf16[128,3584]{1,0:T(8,128)(2,1)S(1)} %shard_map.85.refs_4_), channel_id=1, source_target_pairs={{0,4},{2,6},{4,0},{6,2},{1,5},{3,7},{5,1},{7,3},{8,12},{10,14},{12... | collective-permute-start | bytes 2752520 | tf_op jit(solution)/shard_map/ppermute | solution.py:29
  196.3 26.9 %collective-permute-start.33 = (bf16[128,3584]{1,0:T(8,128)(2,1)S(1)}, bf16[128,3584]{1,0:T(8,128)(2,1)S(1)}, u32[]{:S(2)}, u32[]{:S(2)}) collective-permute-start(bf16[128,3584]{1,0:T(8,128)(2,1)S(1)} %pad_maximum_fusion.1), channel_id=1, source_target_pairs={{0,8},{8,0},{1,9},{9,1},{2,10},{10,2},{3,11},{11,3},{4,12},{12,4},... | collective-permute-start | bytes 2752520 | tf_op jit(solution)/shard_map/ppermute | solution.py:29
  196.4 28.5 %collective-permute-start.38 = (bf16[80,3584]{1,0:T(8,128)(2,1)S(1)}, bf16[80,3584]{1,0:T(8,128)(2,1)S(1)}, u32[]{:S(2)}, u32[]{:S(2)}) collective-permute-start(bf16[80,3584]{1,0:T(8,128)(2,1)S(1)} %get-tuple-element.126), channel_id=1, source_target_pairs={{0,16},{1,17},{8,24},{9,25},{16,0},{17,1},{24,8},{25,9},{2,18},{3,... | collective-permute-start | bytes 1720328 | tf_op jit(solution)/shard_map/ppermute | solution.py:41
  198.1 26.8 %collective-permute-start.39 = (bf16[80,3584]{1,0:T(8,128)(2,1)S(1)}, bf16[80,3584]{1,0:T(8,128)(2,1)S(1)}, u32[]{:S(2)}, u32[]{:S(2)}) collective-permute-start(bf16[80,3584]{1,0:T(8,128)(2,1)S(1)} %get-tuple-element.127), channel_id=1, source_target_pairs={{0,1},{1,0},{8,9},{9,8},{16,17},{17,16},{24,25},{25,24},{2,3},{3,2... | collective-permute-start | bytes 1720328 | tf_op jit(solution)/shard_map/ppermute | solution.py:41
  199.6 25.6 %collective-permute-start.40 = (bf16[80,3584]{1,0:T(8,128)(2,1)S(1)}, bf16[80,3584]{1,0:T(8,128)(2,1)S(1)}, u32[]{:S(2)}, u32[]{:S(2)}) collective-permute-start(bf16[80,3584]{1,0:T(8,128)(2,1)S(1)} %get-tuple-element.128), channel_id=1, source_target_pairs={{0,17},{1,16},{8,25},{9,24},{16,1},{17,0},{24,9},{25,8},{2,19},{3,... | collective-permute-start | bytes 1720328 | tf_op jit(solution)/shard_map/ppermute | solution.py:41
  227.5 25.1 %collective-permute-start.41 = (bf16[128,3584]{1,0:T(8,128)(2,1)S(1)}, bf16[128,3584]{1,0:T(8,128)(2,1)S(1)}, u32[]{:S(2)}, u32[]{:S(2)}) collective-permute-start(bf16[128,3584]{1,0:T(8,128)(2,1)S(1)} %shard_map.89.refs_4_), channel_id=1, source_target_pairs={{0,6},{2,4},{4,2},{6,0},{1,7},{3,5},{5,3},{7,1},{8,14},{10,12},{12... | collective-permute-start | bytes 2752520 | tf_op jit(solution)/shard_map/ppermute | solution.py:29
  232.4 25.1 %collective-permute-start.37 = (bf16[80,3584]{1,0:T(8,128)(2,1)S(1)}, bf16[80,3584]{1,0:T(8,128)(2,1)S(1)}, u32[]{:S(2)}, u32[]{:S(2)}) collective-permute-start(bf16[80,3584]{1,0:T(8,128)(2,1)S(1)} %get-tuple-element.125), channel_id=1, source_target_pairs={{0,17},{1,16},{8,25},{9,24},{16,1},{17,0},{24,9},{25,8},{2,19},{3,... | collective-permute-start | bytes 1720328 | tf_op jit(solution)/shard_map/ppermute | solution.py:41
  233.0 38.4 %collective-permute-start.46 = (bf16[128,3584]{1,0:T(8,128)(2,1)S(1)}, bf16[128,3584]{1,0:T(8,128)(2,1)S(1)}, u32[]{:S(2)}, u32[]{:S(2)}) collective-permute-start(bf16[128,3584]{1,0:T(8,128)(2,1)S(1)} %add_convert_fusion.1), channel_id=1, source_target_pairs={{0,2},{2,0},{4,6},{6,4},{1,3},{3,1},{5,7},{7,5},{8,10},{10,8},{12,... | collective-permute-start | bytes 2752520 | tf_op jit(solution)/shard_map/ppermute | solution.py:29
  (44 other events, 466.8 us)

commit v3 on v2

--- a/solution.py
+++ b/solution.py
@@ -59,7 +59,7 @@
         out_specs=out_specs,
         out_shape=out_shape,
         scratch_shapes=scratch,
-        cost_estimate=pl.CostEstimate(flops=1, bytes_accessed=1, transcendentals=0),
+        cost_estimate=pl.CostEstimate(flops=flops, bytes_accessed=nbytes, transcendentals=0),
         compiler_params=pltpu.CompilerParams(
             dimension_semantics=("arbitrary",), vmem_limit_bytes=limit
         ),
@@ -447,16 +447,16 @@
     have(0, payload_halves)
     dispatch(0)
     up1, down1 = relayed(
-        1, lambda z, u, d: jnp.where(z % 2 == 1, u, d), [up1, down1], 0, 2, *arrived[0]
+        1, lambda z, u, d: jnp.where(z % 2 == 1, u, d), [up1, down1], 0, 2
     )
     up2, down2 = hop(up1, 1, (1, 2)), hop(down1, -1, (1, 2))
-    dispatch(1)
+    dispatch(1, *arrived[0][1:3])
     apply(0)
     (second,) = relayed(
-        2, lambda z, u, d: jnp.where(z >= 2, u, d), [up2, down2], 1, 0, *arrived[1]
+        2, lambda z, u, d: jnp.where(z >= 2, u, d), [up2, down2], 1, 0
     )
     ends = lax.ppermute(second, "plane", [(1, 0), (2, 3)])
-    dispatch(2)
+    dispatch(2, *arrived[1][1:3])
     apply(1)
     relayed(
         3,
@@ -465,7 +465,7 @@
         0,
         0,
     )
-    dispatch(3, *arrived[2])
+    dispatch(3, *arrived[2][1:3])
     apply(2)
     give_back(2)
     apply(3)

time: 276 us -> 262 us (0.949)
  starting transfers between devices: 55.4 us -> 46.2 us
  waiting for transfers between devices: 117 us -> 109 us
    ppermute x18, starting transfers between devices: 16.9 us -> 5.59 us  [swap(): return lax.ppermute(value, axis, [(i, i ^ delta) for i in range(size)])]
    ppermute x4, waiting for transfers between devices: 20.3 us -> 11.9 us  [hop(): return lax.ppermute(value, 'plane', [(z, z + step) for z in sources])]
    ppermute x24, waiting for transfers between devices: 43 us -> 37.9 us  [swap_in_plane(): return lax.ppermute(value, PLANE, pairs)]
    ppermute x18, waiting for transfers between devices: 53.8 us -> 58.4 us  [swap(): return lax.ppermute(value, axis, [(i, i ^ delta) for i in range(size)])]
  transfers between devices with their start and end apart: 47 -> 47, of which waited for: 21 -> 21; matrix products, arithmetic and copies ran while one was open for 1% -> 0% of each run, Pallas kernels for 31% -> 34%
where the time goes in v3:
time: 262 us; the launch traced here: 260 us
  waiting for transfers between devices  109 us (42%)
  Pallas kernels  91 us (35%)
  starting transfers between devices  46.2 us (18%)
  local copies, waits for them, and re-layouts  6.59 us (3%)
  other arithmetic  6.32 us (2%)
    pallas_call x21, Pallas kernels, call(): pl.pallas_call(kernel, grid=grid, in_specs=list(in_specs) + [pl.BlockSpec...  91 us
    ppermute x18, waiting for transfers between devices, swap(): return lax.ppermute(value, axis, [(i, i ^ delta) for i in range(size)])  58.4 us
    ppermute x24, waiting for transfers between devices, swap_in_plane(): return lax.ppermute(value, PLANE, pairs)  37.9 us
    ppermute x24, starting transfers between devices, swap_in_plane(): return lax.ppermute(value, PLANE, pairs)  30.3 us
    ppermute x4, waiting for transfers between devices, hop(): return lax.ppermute(value, 'plane', [(z, z + step) for z in sources])  11.9 us
    ppermute x4, starting transfers between devices, hop(): return lax.ppermute(value, 'plane', [(z, z + step) for z in sources])  8.9 us
    ppermute x18, starting transfers between devices, swap(): return lax.ppermute(value, axis, [(i, i ^ delta) for i in range(size)])  5.59 us
    unnamed x40, local copies, waits for them, and re-layouts  5.49 us
  transfers between devices with their start and end apart: 47, of which 21 were waited for; matrix products, arithmetic and copies ran while one was open for 0% of the time, Pallas kernels for 34%

profile of v3, /device:TPU:0, one launch (start us, length us, event | category | flops | bytes accessed | tf_op | source)
XLA Modules:
  0.0 259.9 jit_solution(9864926761726702451)
XLA Ops:
  3.1 2.2 pad_maximum_fusion
  6.6 5.6 %collective-permute-start.5 = (bf16[144,3584]{1,0:T(8,128)(2,1)}, bf16[144,3584]{1,0:T(8,128)(2,1)S(1)}, u32[]{:S(2)}, u32[]{:S(2)}) collective-permute-start(bf16[144,3584]{1,0:T(8,128)(2,1)} %pad_maximum_fusion), channel_id=1, source_target_pairs={{0,2},{2,4},{4,6},{1,3},{3,5},{5,7},{8,10},{10,12},{12,14},{9,11},... | collective-permute-start | bytes 3096584 | tf_op jit(solution)/shard_map/ppermute | solution.py:387
  15.2 3.2 %shard_map.73 = (bf16[80,3584]{1,0:T(8,128)(2,1)S(1)}, bf16[80,3584]{1,0:T(8,128)(2,1)S(1)}, bf16[80,3584]{1,0:T(8,128)(2,1)S(1)}, bf16[80,3584]{1,0:T(8,128)(2,1)S(1)}, bf16[256,320]{1,0:T(8,128)(2,1)S(1)}) custom-call(f32[320,1]{1,0:T(8,128)S(1)} %add.114.want_ref, bf16[144,1792]{1,0:T(8,128)(2,1)S(1)} %pad_maximum_fusion.2.refs_0_, ...), custom_call_target="tpu_custom_call" | custom-call | flops 587202560 | bytes 4128768 | tf_op jit(solution)/shard_map/pallas_call | solution.py:55
  22.7 10.6 %collective-permute-done.6.refs_1_ = bf16[144,3584]{1,0:T(8,128)(2,1)S(1)} collective-permute-done((bf16[144,3584]{1,0:T(8,128)(2,1)}, bf16[144,3584]{1,0:T(8,128)(2,1)S(1)}, u32[]{:S(2)}, u32[]{:S(2)}) %collective-permute-start.6) | collective-permute-done | bytes 1032224 | tf_op jit(solution)/shard_map/ppermute | solution.py:387
  38.3 2.7 %shard_map.75 = (bf16[80,3584]{1,0:T(8,128)(2,1)S(1)}, bf16[80,3584]{1,0:T(8,128)(2,1)S(1)}, bf16[80,3584]{1,0:T(8,128)(2,1)S(1)}, bf16[80,3584]{1,0:T(8,128)(2,1)}, bf16[256,320]{1,0:T(8,128)(2,1)S(1)}) custom-call(f32[320,1]{1,0:T(8,128)S(1)} %add.114.want_ref, bf16[144,1792]{1,0:T(8,128)(2,1)S(1)} %get-tuple-element.75.refs_0_.refs_4_, ...), custom_call_target="tpu_custom_call" | custom-call | flops 587202560 | bytes 4128768 | tf_op jit(solution)/shard_map/pallas_call | solution.py:55
  44.6 4.2 %collective-permute-done.4.refs_3_ = bf16[80,3584]{1,0:T(8,128)(2,1)S(1)} collective-permute-done((bf16[80,3584]{1,0:T(8,128)(2,1)S(1)}, bf16[80,3584]{1,0:T(8,128)(2,1)S(1)}, u32[]{:S(2)}, u32[]{:S(2)}) %collective-permute-start.4) | collective-permute-done | bytes 573472 | tf_op jit(solution)/shard_map/ppermute | solution.py:41
  48.8 2.9 %collective-permute-start.14 = (bf16[80,3584]{1,0:T(8,128)(2,1)}, bf16[80,3584]{1,0:T(8,128)(2,1)}, u32[]{:S(2)}, u32[]{:S(2)}) collective-permute-start(bf16[80,3584]{1,0:T(8,128)(2,1)} %get-tuple-element.88), channel_id=1, source_target_pairs={{0,17},{1,16},{8,25},{9,24},{16,1},{17,0},{24,9},{25,8},{2,19},{3,... | collective-permute-start | bytes 1720328 | tf_op jit(solution)/shard_map/ppermute | solution.py:41
  51.8 17.2 %shard_map.76 = (bf16[80,3584]{1,0:T(8,128)(2,1)S(1)}, bf16[80,3584]{1,0:T(8,128)(2,1)S(1)}, bf16[80,3584]{1,0:T(8,128)(2,1)S(1)}, bf16[80,3584]{1,0:T(8,128)(2,1)}) custom-call(bf16[80,3584]{1,0:T(8,128)(2,1)} %copy-done.12, bf16[80,3584]{1,0:T(8,128)(2,1)} %copy-done.6, bf16[80,3584]{1,0:T(8,128)(2,1)} %copy-done.7, bf16[80,3584]{1,0:T(8,128)(2,1)} %copy-done.16, ...), custom_call_target="tpu_custom_call" | custom-call | flops 7046430720 | bytes 26607616 | tf_op jit(solution)/shard_map/pallas_call | solution.py:55
  72.9 2.8 %shard_map.78 = (bf16[80,3584]{1,0:T(8,128)(2,1)S(1)}, bf16[80,3584]{1,0:T(8,128)(2,1)}, bf16[80,3584]{1,0:T(8,128)(2,1)}, bf16[80,3584]{1,0:T(8,128)(2,1)}, bf16[256,320]{1,0:T(8,128)(2,1)S(1)}) custom-call(f32[320,1]{1,0:T(8,128)S(1)} %add.114.want_ref, bf16[144,1792]{1,0:T(8,128)(2,1)S(1)} %get-tuple-element.89.refs_0_.refs_4_, ...), custom_call_target="tpu_custom_call" | custom-call | flops 587202560 | bytes 4128768 | tf_op jit(solution)/shard_map/pallas_call | solution.py:55
  79.2 17.3 %shard_map.79 = (bf16[80,3584]{1,0:T(8,128)(2,1)S(1)}, bf16[80,3584]{1,0:T(8,128)(2,1)S(1)}, bf16[80,3584]{1,0:T(8,128)(2,1)S(1)}, bf16[80,3584]{1,0:T(8,128)(2,1)}) custom-call(bf16[80,3584]{1,0:T(8,128)(2,1)} %copy-done.10, bf16[80,3584]{1,0:T(8,128)(2,1)} %copy-done.2, bf16[80,3584]{1,0:T(8,128)(2,1)} %copy-done.3, ...), custom_call_target="tpu_custom_call" | custom-call | flops 7046430720 | bytes 26607616 | tf_op jit(solution)/shard_map/pallas_call | solution.py:55
  100.8 2.6 %shard_map.81 = (bf16[80,3584]{1,0:T(8,128)(2,1)S(1)}, bf16[80,3584]{1,0:T(8,128)(2,1)S(1)}, bf16[80,3584]{1,0:T(8,128)(2,1)}, bf16[80,3584]{1,0:T(8,128)(2,1)S(1)}, bf16[256,320]{1,0:T(8,128)(2,1)S(1)}) custom-call(f32[320,1]{1,0:T(8,128)S(1)} %add.114.want_ref, bf16[144,1792]{1,0:T(8,128)(2,1)S(1)} %get-tuple-element.93.refs_0_.refs_4_, ...), custom_call_target="tpu_custom_call" | custom-call | flops 587202560 | bytes 4128768 | tf_op jit(solution)/shard_map/pallas_call | solution.py:55
  104.9 2.1 collective-permute-start.23
  107.8 17.2 %shard_map.82 = (bf16[80,3584]{1,0:T(8,128)(2,1)S(1)}, bf16[80,3584]{1,0:T(8,128)(2,1)S(1)}, bf16[80,3584]{1,0:T(8,128)(2,1)S(1)}, bf16[80,3584]{1,0:T(8,128)(2,1)}) custom-call(bf16[80,3584]{1,0:T(8,128)(2,1)} %copy-done.11, bf16[80,3584]{1,0:T(8,128)(2,1)} %copy-done.4, bf16[80,3584]{1,0:T(8,128)(2,1)} %copy-done.5, bf16[80,3584]{1,0:T(8,128)(2,1)} %copy-done.15, ...), custom_call_target="tpu_custom_call" | custom-call | flops 7046430720 | bytes 26607616 | tf_op jit(solution)/shard_map/pallas_call | solution.py:55
  127.2 2.1 collective-permute-start.30
  129.3 4.0 %collective-permute-done.23.refs_3_ = bf16[80,3584]{1,0:T(8,128)(2,1)S(1)} collective-permute-done((bf16[80,3584]{1,0:T(8,128)(2,1)S(1)}, bf16[80,3584]{1,0:T(8,128)(2,1)S(1)}, u32[]{:S(2)}, u32[]{:S(2)}) %collective-permute-start.23) | collective-permute-done | bytes 573472 | tf_op jit(solution)/shard_map/ppermute | solution.py:41
  134.2 17.3 %shard_map.83 = (bf16[80,3584]{1,0:T(8,128)(2,1)S(1)}, bf16[80,3584]{1,0:T(8,128)(2,1)S(1)}, bf16[80,3584]{1,0:T(8,128)(2,1)S(1)}, bf16[80,3584]{1,0:T(8,128)(2,1)}) custom-call(bf16[80,3584]{1,0:T(8,128)(2,1)} %copy-done.13, bf16[80,3584]{1,0:T(8,128)(2,1)} %copy-done.17, bf16[80,3584]{1,0:T(8,128)(2,1)} %copy-done.18, bf16[80,3584]{1,0:T(8,128)(2,1)} %copy-done.19, ...), custom_call_target="tpu_custom_call" | custom-call | flops 7046430720 | bytes 26607616 | tf_op jit(solution)/shard_map/pallas_call | solution.py:55
  155.0 3.0 %collective-permute-done.30.refs_3_ = bf16[80,3584]{1,0:T(8,128)(2,1)S(1)} collective-permute-done((bf16[80,3584]{1,0:T(8,128)(2,1)}, bf16[80,3584]{1,0:T(8,128)(2,1)S(1)}, u32[]{:S(2)}, u32[]{:S(2)}) %collective-permute-start.30) | collective-permute-done | bytes 573472 | tf_op jit(solution)/shard_map/ppermute | solution.py:41
  163.8 6.4 %collective-permute-done.25.refs_1_ = bf16[80,3584]{1,0:T(8,128)(2,1)S(1)} collective-permute-done((bf16[80,3584]{1,0:T(8,128)(2,1)S(1)}, bf16[80,3584]{1,0:T(8,128)(2,1)S(1)}, u32[]{:S(2)}, u32[]{:S(2)}) %collective-permute-start.25) | collective-permute-done | bytes 573472 | tf_op jit(solution)/shard_map/ppermute | solution.py:41
  170.2 11.2 %collective-permute-done.27.refs_3_ = bf16[80,3584]{1,0:T(8,128)(2,1)S(1)} collective-permute-done((bf16[80,3584]{1,0:T(8,128)(2,1)}, bf16[80,3584]{1,0:T(8,128)(2,1)S(1)}, u32[]{:S(2)}, u32[]{:S(2)}) %collective-permute-start.27) | collective-permute-done | bytes 573472 | tf_op jit(solution)/shard_map/ppermute | solution.py:41
  186.8 18.6 %collective-permute-done.34.refs_2_ = bf16[128,3584]{1,0:T(8,128)(2,1)S(1)} collective-permute-done((bf16[128,3584]{1,0:T(8,128)(2,1)S(1)}, bf16[128,3584]{1,0:T(8,128)(2,1)S(1)}, u32[]{:S(2)}, u32[]{:S(2)}) %collective-permute-start.34) | collective-permute-done | bytes 917536 | tf_op jit(solution)/shard_map/ppermute | solution.py:29
  207.2 5.0 %collective-permute-done.40.refs_3_ = bf16[80,3584]{1,0:T(8,128)(2,1)S(1)} collective-permute-done((bf16[80,3584]{1,0:T(8,128)(2,1)S(1)}, bf16[80,3584]{1,0:T(8,128)(2,1)S(1)}, u32[]{:S(2)}, u32[]{:S(2)}) %collective-permute-start.40) | collective-permute-done | bytes 573472 | tf_op jit(solution)/shard_map/ppermute | solution.py:41
  219.2 20.3 %collective-permute-done.41.refs_2_ = bf16[128,3584]{1,0:T(8,128)(2,1)S(1)} collective-permute-done((bf16[128,3584]{1,0:T(8,128)(2,1)S(1)}, bf16[128,3584]{1,0:T(8,128)(2,1)S(1)}, u32[]{:S(2)}, u32[]{:S(2)}) %collective-permute-start.41) | collective-permute-done | bytes 917536 | tf_op jit(solution)/shard_map/ppermute | solution.py:29
  239.6 3.5 %collective-permute-done.37.refs_3_ = bf16[80,3584]{1,0:T(8,128)(2,1)S(1)} collective-permute-done((bf16[80,3584]{1,0:T(8,128)(2,1)S(1)}, bf16[80,3584]{1,0:T(8,128)(2,1)S(1)}, u32[]{:S(2)}, u32[]{:S(2)}) %collective-permute-start.37) | collective-permute-done | bytes 573472 | tf_op jit(solution)/shard_map/ppermute | solution.py:41
  245.4 13.0 %collective-permute-done.46 = bf16[128,3584]{1,0:T(8,128)(2,1)S(1)} collective-permute-done((bf16[128,3584]{1,0:T(8,128)(2,1)S(1)}, bf16[128,3584]{1,0:T(8,128)(2,1)S(1)}, u32[]{:S(2)}, u32[]{:S(2)}) %collective-permute-start.46) | collective-permute-done | bytes 917536 | tf_op jit(solution)/shard_map/ppermute | solution.py:29
  (153 shorter events, 64.4 us)
Async XLA Ops:
  5.3 27.9 %collective-permute-start.6 = (bf16[144,3584]{1,0:T(8,128)(2,1)}, bf16[144,3584]{1,0:T(8,128)(2,1)S(1)}, u32[]{:S(2)}, u32[]{:S(2)}) collective-permute-start(bf16[144,3584]{1,0:T(8,128)(2,1)} %pad_maximum_fusion), channel_id=1, source_target_pairs={{2,0},{4,2},{6,4},{3,1},{5,3},{7,5},{10,8},{12,10},{14,12},{11,9},... | collective-permute-start | bytes 3096584 | tf_op jit(solution)/shard_map/ppermute | solution.py:387
  6.6 27.9 %collective-permute-start.5 = (bf16[144,3584]{1,0:T(8,128)(2,1)}, bf16[144,3584]{1,0:T(8,128)(2,1)S(1)}, u32[]{:S(2)}, u32[]{:S(2)}) collective-permute-start(bf16[144,3584]{1,0:T(8,128)(2,1)} %pad_maximum_fusion), channel_id=1, source_target_pairs={{0,2},{2,4},{4,6},{1,3},{3,5},{5,7},{8,10},{10,12},{12,14},{9,11},... | collective-permute-start | bytes 3096584 | tf_op jit(solution)/shard_map/ppermute | solution.py:387
  22.6 26.2 %collective-permute-start.4 = (bf16[80,3584]{1,0:T(8,128)(2,1)S(1)}, bf16[80,3584]{1,0:T(8,128)(2,1)S(1)}, u32[]{:S(2)}, u32[]{:S(2)}) collective-permute-start(bf16[80,3584]{1,0:T(8,128)(2,1)S(1)} %get-tuple-element.74), channel_id=1, source_target_pairs={{0,17},{1,16},{8,25},{9,24},{16,1},{17,0},{24,9},{25,8},{2,19},{3,... | collective-permute-start | bytes 1720328 | tf_op jit(solution)/shard_map/ppermute | solution.py:41
  35.8 33.1 %collective-permute-start.9 = (bf16[144,3584]{1,0:T(8,128)(2,1)S(1)}, bf16[144,3584]{1,0:T(8,128)(2,1)S(1)}, u32[]{:S(2)}, u32[]{:S(2)}) collective-permute-start(bf16[144,3584]{1,0:T(8,128)(2,1)S(1)} %get-tuple-element.82.refs_0_), channel_id=1, source_target_pairs={{2,4},{4,6},{3,5},{5,7},{10,12},{12,14},{11,13},{13,15},{18,20},{2... | collective-permute-start | bytes 3096584 | tf_op jit(solution)/shard_map/ppermute | solution.py:387
  37.0 32.0 %collective-permute-start.10 = (bf16[144,3584]{1,0:T(8,128)(2,1)S(1)}, bf16[144,3584]{1,0:T(8,128)(2,1)S(1)}, u32[]{:S(2)}, u32[]{:S(2)}) collective-permute-start(bf16[144,3584]{1,0:T(8,128)(2,1)S(1)} %get-tuple-element.83.refs_1_), channel_id=1, source_target_pairs={{2,0},{4,2},{3,1},{5,3},{10,8},{12,10},{11,9},{13,11},{18,16},{20,... | collective-permute-start | bytes 3096584 | tf_op jit(solution)/shard_map/ppermute | solution.py:387
  41.8 29.0 %collective-permute-start.12 = (bf16[80,3584]{1,0:T(8,128)(2,1)S(1)}, bf16[80,3584]{1,0:T(8,128)(2,1)S(1)}, u32[]{:S(2)}, u32[]{:S(2)}) collective-permute-start(bf16[80,3584]{1,0:T(8,128)(2,1)S(1)} %get-tuple-element.86), channel_id=1, source_target_pairs={{0,16},{1,17},{8,24},{9,25},{16,0},{17,1},{24,8},{25,9},{2,18},{3,... | collective-permute-start | bytes 1720328 | tf_op jit(solution)/shard_map/ppermute | solution.py:41
  43.1 29.2 %collective-permute-start.13 = (bf16[80,3584]{1,0:T(8,128)(2,1)S(1)}, bf16[80,3584]{1,0:T(8,128)(2,1)S(1)}, u32[]{:S(2)}, u32[]{:S(2)}) collective-permute-start(bf16[80,3584]{1,0:T(8,128)(2,1)S(1)} %get-tuple-element.87), channel_id=1, source_target_pairs={{0,1},{1,0},{8,9},{9,8},{16,17},{17,16},{24,25},{25,24},{2,3},{3,2... | collective-permute-start | bytes 1720328 | tf_op jit(solution)/shard_map/ppermute | solution.py:41
  48.8 30.4 %collective-permute-start.14 = (bf16[80,3584]{1,0:T(8,128)(2,1)}, bf16[80,3584]{1,0:T(8,128)(2,1)}, u32[]{:S(2)}, u32[]{:S(2)}) collective-permute-start(bf16[80,3584]{1,0:T(8,128)(2,1)} %get-tuple-element.88), channel_id=1, source_target_pairs={{0,17},{1,16},{8,25},{9,24},{16,1},{17,0},{24,9},{25,8},{2,19},{3,... | collective-permute-start | bytes 1720328 | tf_op jit(solution)/shard_map/ppermute | solution.py:41
  70.8 26.8 %collective-permute-start.11 = (bf16[144,3584]{1,0:T(8,128)(2,1)}, bf16[144,3584]{1,0:T(8,128)(2,1)S(1)}, u32[]{:S(2)}, u32[]{:S(2)}) collective-permute-start(bf16[144,3584]{1,0:T(8,128)(2,1)} %get-tuple-element.84), channel_id=1, source_target_pairs={{2,0},{4,6},{3,1},{5,7},{10,8},{12,14},{11,9},{13,15},{18,16},{20,... | collective-permute-start | bytes 3096584 | tf_op jit(solution)/shard_map/ppermute | solution.py:458
  77.2 29.9 %collective-permute-start.24 = (bf16[80,3584]{1,0:T(8,128)(2,1)}, bf16[80,3584]{1,0:T(8,128)(2,1)S(1)}, u32[]{:S(2)}, u32[]{:S(2)}) collective-permute-start(bf16[80,3584]{1,0:T(8,128)(2,1)} %get-tuple-element.103), channel_id=1, source_target_pairs={{0,17},{1,16},{8,25},{9,24},{16,1},{17,0},{24,9},{25,8},{2,19},{3,... | collective-permute-start | bytes 1720328 | tf_op jit(solution)/shard_map/ppermute | solution.py:41
  104.0 25.4 %collective-permute-start.22 = (bf16[80,3584]{1,0:T(8,128)(2,1)}, bf16[80,3584]{1,0:T(8,128)(2,1)S(1)}, u32[]{:S(2)}, u32[]{:S(2)}) collective-permute-start(bf16[80,3584]{1,0:T(8,128)(2,1)} %get-tuple-element.100), channel_id=1, source_target_pairs={{0,1},{1,0},{8,9},{9,8},{16,17},{17,16},{24,25},{25,24},{2,3},{3,2... | collective-permute-start | bytes 1720328 | tf_op jit(solution)/shard_map/ppermute | solution.py:41
  104.9 28.5 %collective-permute-start.23 = (bf16[80,3584]{1,0:T(8,128)(2,1)S(1)}, bf16[80,3584]{1,0:T(8,128)(2,1)S(1)}, u32[]{:S(2)}, u32[]{:S(2)}) collective-permute-start(bf16[80,3584]{1,0:T(8,128)(2,1)S(1)} %get-tuple-element.101), channel_id=1, source_target_pairs={{0,17},{1,16},{8,25},{9,24},{16,1},{17,0},{24,9},{25,8},{2,19},{3,... | collective-permute-start | bytes 1720328 | tf_op jit(solution)/shard_map/ppermute | solution.py:41
  125.8 27.0 %collective-permute-start.28 = (bf16[80,3584]{1,0:T(8,128)(2,1)S(1)}, bf16[80,3584]{1,0:T(8,128)(2,1)S(1)}, u32[]{:S(2)}, u32[]{:S(2)}) collective-permute-start(bf16[80,3584]{1,0:T(8,128)(2,1)S(1)} %get-tuple-element.112), channel_id=1, source_target_pairs={{0,16},{1,17},{8,24},{9,25},{16,0},{17,1},{24,8},{25,9},{2,18},{3,... | collective-permute-start | bytes 1720328 | tf_op jit(solution)/shard_map/ppermute | solution.py:41
  126.3 28.7 %collective-permute-start.29 = (bf16[80,3584]{1,0:T(8,128)(2,1)S(1)}, bf16[80,3584]{1,0:T(8,128)(2,1)S(1)}, u32[]{:S(2)}, u32[]{:S(2)}) collective-permute-start(bf16[80,3584]{1,0:T(8,128)(2,1)S(1)} %get-tuple-element.113), channel_id=1, source_target_pairs={{0,1},{1,0},{8,9},{9,8},{16,17},{17,16},{24,25},{25,24},{2,3},{3,2... | collective-permute-start | bytes 1720328 | tf_op jit(solution)/shard_map/ppermute | solution.py:41
  127.2 30.8 %collective-permute-start.30 = (bf16[80,3584]{1,0:T(8,128)(2,1)}, bf16[80,3584]{1,0:T(8,128)(2,1)S(1)}, u32[]{:S(2)}, u32[]{:S(2)}) collective-permute-start(bf16[80,3584]{1,0:T(8,128)(2,1)} %get-tuple-element.114), channel_id=1, source_target_pairs={{0,17},{1,16},{8,25},{9,24},{16,1},{17,0},{24,9},{25,8},{2,19},{3,... | collective-permute-start | bytes 1720328 | tf_op jit(solution)/shard_map/ppermute | solution.py:41
  152.9 28.6 %collective-permute-start.27 = (bf16[80,3584]{1,0:T(8,128)(2,1)}, bf16[80,3584]{1,0:T(8,128)(2,1)S(1)}, u32[]{:S(2)}, u32[]{:S(2)}) collective-permute-start(bf16[80,3584]{1,0:T(8,128)(2,1)} %get-tuple-element.108), channel_id=1, source_target_pairs={{0,17},{1,16},{8,25},{9,24},{16,1},{17,0},{24,9},{25,8},{2,19},{3,... | collective-permute-start | bytes 1720328 | tf_op jit(solution)/shard_map/ppermute | solution.py:41
  162.4 43.0 %collective-permute-start.34 = (bf16[128,3584]{1,0:T(8,128)(2,1)S(1)}, bf16[128,3584]{1,0:T(8,128)(2,1)S(1)}, u32[]{:S(2)}, u32[]{:S(2)}) collective-permute-start(bf16[128,3584]{1,0:T(8,128)(2,1)S(1)} %shard_map.85.refs_4_), channel_id=1, source_target_pairs={{0,4},{2,6},{4,0},{6,2},{1,5},{3,7},{5,1},{7,3},{8,12},{10,14},{12... | collective-permute-start | bytes 2752520 | tf_op jit(solution)/shard_map/ppermute | solution.py:29
  183.3 23.9 %collective-permute-start.38 = (bf16[80,3584]{1,0:T(8,128)(2,1)S(1)}, bf16[80,3584]{1,0:T(8,128)(2,1)S(1)}, u32[]{:S(2)}, u32[]{:S(2)}) collective-permute-start(bf16[80,3584]{1,0:T(8,128)(2,1)S(1)} %get-tuple-element.126), channel_id=1, source_target_pairs={{0,16},{1,17},{8,24},{9,25},{16,0},{17,1},{24,8},{25,9},{2,18},{3,... | collective-permute-start | bytes 1720328 | tf_op jit(solution)/shard_map/ppermute | solution.py:41
  184.8 27.4 %collective-permute-start.40 = (bf16[80,3584]{1,0:T(8,128)(2,1)S(1)}, bf16[80,3584]{1,0:T(8,128)(2,1)S(1)}, u32[]{:S(2)}, u32[]{:S(2)}) collective-permute-start(bf16[80,3584]{1,0:T(8,128)(2,1)S(1)} %get-tuple-element.128), channel_id=1, source_target_pairs={{0,17},{1,16},{8,25},{9,24},{16,1},{17,0},{24,9},{25,8},{2,19},{3,... | collective-permute-start | bytes 1720328 | tf_op jit(solution)/shard_map/ppermute | solution.py:41
  214.4 25.1 %collective-permute-start.41 = (bf16[128,3584]{1,0:T(8,128)(2,1)S(1)}, bf16[128,3584]{1,0:T(8,128)(2,1)S(1)}, u32[]{:S(2)}, u32[]{:S(2)}) collective-permute-start(bf16[128,3584]{1,0:T(8,128)(2,1)S(1)} %shard_map.89.refs_4_), channel_id=1, source_target_pairs={{0,6},{2,4},{4,2},{6,0},{1,7},{3,5},{5,3},{7,1},{8,14},{10,12},{12... | collective-permute-start | bytes 2752520 | tf_op jit(solution)/shard_map/ppermute | solution.py:29
  214.9 24.6 %collective-permute-start.35 = (bf16[80,3584]{1,0:T(8,128)(2,1)S(1)}, bf16[80,3584]{1,0:T(8,128)(2,1)S(1)}, u32[]{:S(2)}, u32[]{:S(2)}) collective-permute-start(bf16[80,3584]{1,0:T(8,128)(2,1)S(1)} %get-tuple-element.123), channel_id=1, source_target_pairs={{0,16},{1,17},{8,24},{9,25},{16,0},{17,1},{24,8},{25,9},{2,18},{3,... | collective-permute-start | bytes 1720328 | tf_op jit(solution)/shard_map/ppermute | solution.py:41
  215.7 23.9 %collective-permute-start.36 = (bf16[80,3584]{1,0:T(8,128)(2,1)S(1)}, bf16[80,3584]{1,0:T(8,128)(2,1)S(1)}, u32[]{:S(2)}, u32[]{:S(2)}) collective-permute-start(bf16[80,3584]{1,0:T(8,128)(2,1)S(1)} %get-tuple-element.124), channel_id=1, source_target_pairs={{0,1},{1,0},{8,9},{9,8},{16,17},{17,16},{24,25},{25,24},{2,3},{3,2... | collective-permute-start | bytes 1720328 | tf_op jit(solution)/shard_map/ppermute | solution.py:41
  217.2 25.9 %collective-permute-start.37 = (bf16[80,3584]{1,0:T(8,128)(2,1)S(1)}, bf16[80,3584]{1,0:T(8,128)(2,1)S(1)}, u32[]{:S(2)}, u32[]{:S(2)}) collective-permute-start(bf16[80,3584]{1,0:T(8,128)(2,1)S(1)} %get-tuple-element.125), channel_id=1, source_target_pairs={{0,17},{1,16},{8,25},{9,24},{16,1},{17,0},{24,9},{25,8},{2,19},{3,... | collective-permute-start | bytes 1720328 | tf_op jit(solution)/shard_map/ppermute | solution.py:41
  218.6 39.7 %collective-permute-start.46 = (bf16[128,3584]{1,0:T(8,128)(2,1)S(1)}, bf16[128,3584]{1,0:T(8,128)(2,1)S(1)}, u32[]{:S(2)}, u32[]{:S(2)}) collective-permute-start(bf16[128,3584]{1,0:T(8,128)(2,1)S(1)} %add_convert_fusion.1), channel_id=1, source_target_pairs={{0,2},{2,0},{4,6},{6,4},{1,3},{3,1},{5,7},{7,5},{8,10},{10,8},{12,... | collective-permute-start | bytes 2752520 | tf_op jit(solution)/shard_map/ppermute | solution.py:29
  (43 other events, 369.1 us)

commit v4 on v3

--- a/solution.py
+++ b/solution.py
@@ -450,13 +450,13 @@
         1, lambda z, u, d: jnp.where(z % 2 == 1, u, d), [up1, down1], 0, 2
     )
     up2, down2 = hop(up1, 1, (1, 2)), hop(down1, -1, (1, 2))
-    dispatch(1, *arrived[0][1:3])
+    dispatch(1, arrived[0][1])
     apply(0)
     (second,) = relayed(
         2, lambda z, u, d: jnp.where(z >= 2, u, d), [up2, down2], 1, 0
     )
     ends = lax.ppermute(second, "plane", [(1, 0), (2, 3)])
-    dispatch(2, *arrived[1][1:3])
+    dispatch(2, arrived[1][1])
     apply(1)
     relayed(
         3,
@@ -465,7 +465,7 @@
         0,
         0,
     )
-    dispatch(3, *arrived[2][1:3])
+    dispatch(3, arrived[2][1])
     apply(2)
     give_back(2)
     apply(3)

time: 262 us -> 277 us (1.057)
  waiting for transfers between devices: 109 us -> 118 us
  starting transfers between devices: 46.2 us -> 54.1 us
    ppermute x24, waiting for transfers between devices: 37.9 us -> 50.6 us  [swap_in_plane(): return lax.ppermute(value, PLANE, pairs)]
    ppermute x18, starting transfers between devices: 5.59 us -> 14 us  [swap(): return lax.ppermute(value, axis, [(i, i ^ delta) for i in range(size)])]
    ppermute x18, waiting for transfers between devices: 58.4 us -> 53.4 us  [swap(): return lax.ppermute(value, axis, [(i, i ^ delta) for i in range(size)])]
  transfers between devices with their start and end apart: 47 -> 47, of which waited for: 21 -> 22; matrix products, arithmetic and copies ran while one was open for 0% -> 0% of each run, Pallas kernels for 34% -> 32%
where the time goes in v4:
time: 277 us; the launch traced here: 274 us
  waiting for transfers between devices  118 us (43%)
  Pallas kernels  89.5 us (32%)
  starting transfers between devices  54.1 us (20%)
  other arithmetic  6.38 us (2%)
  local copies, waits for them, and re-layouts  4.45 us (2%)
    pallas_call x21, Pallas kernels, call(): pl.pallas_call(kernel, grid=grid, in_specs=list(in_specs) + [pl.BlockSpec...  89.5 us
    ppermute x18, waiting for transfers between devices, swap(): return lax.ppermute(value, axis, [(i, i ^ delta) for i in range(size)])  53.4 us
    ppermute x24, waiting for transfers between devices, swap_in_plane(): return lax.ppermute(value, PLANE, pairs)  50.6 us
    ppermute x24, starting transfers between devices, swap_in_plane(): return lax.ppermute(value, PLANE, pairs)  29.7 us
    ppermute x4, waiting for transfers between devices, hop(): return lax.ppermute(value, 'plane', [(z, z + step) for z in sources])  14.1 us
    ppermute x18, starting transfers between devices, swap(): return lax.ppermute(value, axis, [(i, i ^ delta) for i in range(size)])  14 us
    ppermute x4, starting transfers between devices, hop(): return lax.ppermute(value, 'plane', [(z, z + step) for z in sources])  8.92 us
  transfers between devices with their start and end apart: 47, of which 22 were waited for; matrix products, arithmetic and copies ran while one was open for 0% of the time, Pallas kernels for 32%

profile of v4, /device:TPU:0, one launch (start us, length us, event | category | flops | bytes accessed | tf_op | source)
XLA Modules:
  0.0 273.5 jit_solution(15863120177631876118)
XLA Ops:
  3.1 2.3 pad_maximum_fusion
  6.6 5.6 %collective-permute-start.5 = (bf16[144,3584]{1,0:T(8,128)(2,1)}, bf16[144,3584]{1,0:T(8,128)(2,1)S(1)}, u32[]{:S(2)}, u32[]{:S(2)}) collective-permute-start(bf16[144,3584]{1,0:T(8,128)(2,1)} %pad_maximum_fusion), channel_id=1, source_target_pairs={{0,2},{2,4},{4,6},{1,3},{3,5},{5,7},{8,10},{10,12},{12,14},{9,11},... | collective-permute-start | bytes 3096584 | tf_op jit(solution)/shard_map/ppermute | solution.py:387
  15.2 3.2 %shard_map.73 = (bf16[80,3584]{1,0:T(8,128)(2,1)S(1)}, bf16[80,3584]{1,0:T(8,128)(2,1)S(1)}, bf16[80,3584]{1,0:T(8,128)(2,1)S(1)}, bf16[80,3584]{1,0:T(8,128)(2,1)S(1)}, bf16[256,320]{1,0:T(8,128)(2,1)S(1)}) custom-call(f32[320,1]{1,0:T(8,128)S(1)} %add.114.want_ref, bf16[144,1792]{1,0:T(8,128)(2,1)S(1)} %pad_maximum_fusion.2.refs_0_, ...), custom_call_target="tpu_custom_call" | custom-call | flops 587202560 | bytes 4128768 | tf_op jit(solution)/shard_map/pallas_call | solution.py:55
  18.4 2.0 collective-permute-start.2
  20.5 12.8 %collective-permute-done.6.refs_1_ = bf16[144,3584]{1,0:T(8,128)(2,1)S(1)} collective-permute-done((bf16[144,3584]{1,0:T(8,128)(2,1)}, bf16[144,3584]{1,0:T(8,128)(2,1)S(1)}, u32[]{:S(2)}, u32[]{:S(2)}) %collective-permute-start.6) | collective-permute-done | bytes 1032224 | tf_op jit(solution)/shard_map/ppermute | solution.py:387
  40.6 2.7 shard_map.75
  43.7 7.6 %collective-permute-done.3.refs_2_ = bf16[80,3584]{1,0:T(8,128)(2,1)S(1)} collective-permute-done((bf16[80,3584]{1,0:T(8,128)(2,1)S(1)}, bf16[80,3584]{1,0:T(8,128)(2,1)S(1)}, u32[]{:S(2)}, u32[]{:S(2)}) %collective-permute-start.3) | collective-permute-done | bytes 573472 | tf_op jit(solution)/shard_map/ppermute | solution.py:41
  52.9 11.8 %collective-permute-done.4.refs_3_ = bf16[80,3584]{1,0:T(8,128)(2,1)S(1)} collective-permute-done((bf16[80,3584]{1,0:T(8,128)(2,1)S(1)}, bf16[80,3584]{1,0:T(8,128)(2,1)S(1)}, u32[]{:S(2)}, u32[]{:S(2)}) %collective-permute-start.4) | collective-permute-done | bytes 573472 | tf_op jit(solution)/shard_map/ppermute | solution.py:41
  66.1 17.3 %shard_map.76 = (bf16[80,3584]{1,0:T(8,128)(2,1)S(1)}, bf16[80,3584]{1,0:T(8,128)(2,1)S(1)}, bf16[80,3584]{1,0:T(8,128)(2,1)S(1)}, bf16[80,3584]{1,0:T(8,128)(2,1)}) custom-call(bf16[80,3584]{1,0:T(8,128)(2,1)} %copy-done.9, bf16[80,3584]{1,0:T(8,128)(2,1)} %copy-done.2, bf16[80,3584]{1,0:T(8,128)(2,1)} %copy-done.12, bf16[80,3584]{1,0:T(8,128)(2,1)} %copy-done.13, ...), custom_call_target="tpu_custom_call" | custom-call | flops 7046430720 | bytes 26607616 | tf_op jit(solution)/shard_map/pallas_call | solution.py:55
  86.6 2.7 shard_map.78
  93.6 17.2 %shard_map.79 = (bf16[80,3584]{1,0:T(8,128)(2,1)S(1)}, bf16[80,3584]{1,0:T(8,128)(2,1)S(1)}, bf16[80,3584]{1,0:T(8,128)(2,1)S(1)}, bf16[80,3584]{1,0:T(8,128)(2,1)}) custom-call(bf16[80,3584]{1,0:T(8,128)(2,1)} %copy-done.7, bf16[80,3584]{1,0:T(8,128)(2,1)} %copy-done, bf16[80,3584]{1,0:T(8,128)(2,1)} %collective-permute-done.13.refs_2_, ...), custom_call_target="tpu_custom_call" | custom-call | flops 7046430720 | bytes 26607616 | tf_op jit(solution)/shard_map/pallas_call | solution.py:55
  120.0 17.2 %shard_map.82 = (bf16[80,3584]{1,0:T(8,128)(2,1)S(1)}, bf16[80,3584]{1,0:T(8,128)(2,1)S(1)}, bf16[80,3584]{1,0:T(8,128)(2,1)S(1)}, bf16[80,3584]{1,0:T(8,128)(2,1)}) custom-call(bf16[80,3584]{1,0:T(8,128)(2,1)} %copy-done.8, bf16[80,3584]{1,0:T(8,128)(2,1)} %copy-done.1, bf16[80,3584]{1,0:T(8,128)(2,1)} %collective-permute-done.23.refs_2_, ...), custom_call_target="tpu_custom_call" | custom-call | flops 7046430720 | bytes 26607616 | tf_op jit(solution)/shard_map/pallas_call | solution.py:55
  142.3 3.9 %collective-permute-done.22.refs_3_ = bf16[80,3584]{1,0:T(8,128)(2,1)} collective-permute-done((bf16[80,3584]{1,0:T(8,128)(2,1)S(1)}, bf16[80,3584]{1,0:T(8,128)(2,1)}, u32[]{:S(2)}, u32[]{:S(2)}) %collective-permute-start.22) | collective-permute-done | bytes 573472 | tf_op jit(solution)/shard_map/ppermute | solution.py:41
  146.2 17.3 %shard_map.83 = (bf16[80,3584]{1,0:T(8,128)(2,1)S(1)}, bf16[80,3584]{1,0:T(8,128)(2,1)S(1)}, bf16[80,3584]{1,0:T(8,128)(2,1)S(1)}, bf16[80,3584]{1,0:T(8,128)(2,1)}) custom-call(bf16[80,3584]{1,0:T(8,128)(2,1)} %copy-done.10, bf16[80,3584]{1,0:T(8,128)(2,1)} %copy-done.14, bf16[80,3584]{1,0:T(8,128)(2,1)} %copy-done.15, ...), custom_call_target="tpu_custom_call" | custom-call | flops 7046430720 | bytes 26607616 | tf_op jit(solution)/shard_map/pallas_call | solution.py:55
  167.0 3.7 %collective-permute-done.30.refs_3_ = bf16[80,3584]{1,0:T(8,128)(2,1)S(1)} collective-permute-done((bf16[80,3584]{1,0:T(8,128)(2,1)}, bf16[80,3584]{1,0:T(8,128)(2,1)S(1)}, u32[]{:S(2)}, u32[]{:S(2)}) %collective-permute-start.30) | collective-permute-done | bytes 573472 | tf_op jit(solution)/shard_map/ppermute | solution.py:41
  175.1 4.9 %collective-permute-start.34 = (bf16[128,3584]{1,0:T(8,128)(2,1)S(1)}, bf16[128,3584]{1,0:T(8,128)(2,1)S(1)}, u32[]{:S(2)}, u32[]{:S(2)}) collective-permute-start(bf16[128,3584]{1,0:T(8,128)(2,1)S(1)} %shard_map.85.refs_4_), channel_id=1, source_target_pairs={{0,4},{2,6},{4,0},{6,2},{1,5},{3,7},{5,1},{7,3},{8,12},{10,14},{12... | collective-permute-start | bytes 2752520 | tf_op jit(solution)/shard_map/ppermute | solution.py:29
  180.6 2.4 collective-permute-done.25.refs_1_
  183.1 11.1 %collective-permute-done.27.refs_3_ = bf16[80,3584]{1,0:T(8,128)(2,1)S(1)} collective-permute-done((bf16[80,3584]{1,0:T(8,128)(2,1)}, bf16[80,3584]{1,0:T(8,128)(2,1)S(1)}, u32[]{:S(2)}, u32[]{:S(2)}) %collective-permute-start.27) | collective-permute-done | bytes 573472 | tf_op jit(solution)/shard_map/ppermute | solution.py:41
  199.6 20.4 %collective-permute-done.34.refs_2_ = bf16[128,3584]{1,0:T(8,128)(2,1)S(1)} collective-permute-done((bf16[128,3584]{1,0:T(8,128)(2,1)S(1)}, bf16[128,3584]{1,0:T(8,128)(2,1)S(1)}, u32[]{:S(2)}, u32[]{:S(2)}) %collective-permute-start.34) | collective-permute-done | bytes 917536 | tf_op jit(solution)/shard_map/ppermute | solution.py:29
  221.7 3.2 %collective-permute-done.40.refs_3_ = bf16[80,3584]{1,0:T(8,128)(2,1)S(1)} collective-permute-done((bf16[80,3584]{1,0:T(8,128)(2,1)S(1)}, bf16[80,3584]{1,0:T(8,128)(2,1)S(1)}, u32[]{:S(2)}, u32[]{:S(2)}) %collective-permute-start.40) | collective-permute-done | bytes 573472 | tf_op jit(solution)/shard_map/ppermute | solution.py:41
  227.2 4.4 %collective-permute-start.41 = (bf16[128,3584]{1,0:T(8,128)(2,1)S(1)}, bf16[128,3584]{1,0:T(8,128)(2,1)S(1)}, u32[]{:S(2)}, u32[]{:S(2)}) collective-permute-start(bf16[128,3584]{1,0:T(8,128)(2,1)S(1)} %shard_map.89.refs_4_), channel_id=1, source_target_pairs={{0,6},{2,4},{4,2},{6,0},{1,7},{3,5},{5,3},{7,1},{8,14},{10,12},{12... | collective-permute-start | bytes 2752520 | tf_op jit(solution)/shard_map/ppermute | solution.py:29
  236.3 16.5 %collective-permute-done.41.refs_2_ = bf16[128,3584]{1,0:T(8,128)(2,1)S(1)} collective-permute-done((bf16[128,3584]{1,0:T(8,128)(2,1)S(1)}, bf16[128,3584]{1,0:T(8,128)(2,1)S(1)}, u32[]{:S(2)}, u32[]{:S(2)}) %collective-permute-start.41) | collective-permute-done | bytes 917536 | tf_op jit(solution)/shard_map/ppermute | solution.py:29
  252.9 6.8 %collective-permute-done.37.refs_3_ = bf16[80,3584]{1,0:T(8,128)(2,1)S(1)} collective-permute-done((bf16[80,3584]{1,0:T(8,128)(2,1)S(1)}, bf16[80,3584]{1,0:T(8,128)(2,1)S(1)}, u32[]{:S(2)}, u32[]{:S(2)}) %collective-permute-start.37) | collective-permute-done | bytes 573472 | tf_op jit(solution)/shard_map/ppermute | solution.py:41
  262.1 9.9 %collective-permute-done.46 = bf16[128,3584]{1,0:T(8,128)(2,1)S(1)} collective-permute-done((bf16[128,3584]{1,0:T(8,128)(2,1)S(1)}, bf16[128,3584]{1,0:T(8,128)(2,1)S(1)}, u32[]{:S(2)}, u32[]{:S(2)}) %collective-permute-start.46) | collective-permute-done | bytes 917536 | tf_op jit(solution)/shard_map/ppermute | solution.py:29
  (145 shorter events, 66.0 us)
Async XLA Ops:
  5.4 27.9 %collective-permute-start.6 = (bf16[144,3584]{1,0:T(8,128)(2,1)}, bf16[144,3584]{1,0:T(8,128)(2,1)S(1)}, u32[]{:S(2)}, u32[]{:S(2)}) collective-permute-start(bf16[144,3584]{1,0:T(8,128)(2,1)} %pad_maximum_fusion), channel_id=1, source_target_pairs={{2,0},{4,2},{6,4},{3,1},{5,3},{7,5},{10,8},{12,10},{14,12},{11,9},... | collective-permute-start | bytes 3096584 | tf_op jit(solution)/shard_map/ppermute | solution.py:387
  6.6 27.9 %collective-permute-start.5 = (bf16[144,3584]{1,0:T(8,128)(2,1)}, bf16[144,3584]{1,0:T(8,128)(2,1)S(1)}, u32[]{:S(2)}, u32[]{:S(2)}) collective-permute-start(bf16[144,3584]{1,0:T(8,128)(2,1)} %pad_maximum_fusion), channel_id=1, source_target_pairs={{0,2},{2,4},{4,6},{1,3},{3,5},{5,7},{8,10},{10,12},{12,14},{9,11},... | collective-permute-start | bytes 3096584 | tf_op jit(solution)/shard_map/ppermute | solution.py:387
  37.1 27.6 %collective-permute-start.4 = (bf16[80,3584]{1,0:T(8,128)(2,1)S(1)}, bf16[80,3584]{1,0:T(8,128)(2,1)S(1)}, u32[]{:S(2)}, u32[]{:S(2)}) collective-permute-start(bf16[80,3584]{1,0:T(8,128)(2,1)S(1)} %get-tuple-element.74), channel_id=1, source_target_pairs={{0,17},{1,16},{8,25},{9,24},{16,1},{17,0},{24,9},{25,8},{2,19},{3,... | collective-permute-start | bytes 1720328 | tf_op jit(solution)/shard_map/ppermute | solution.py:41
  38.6 44.8 %collective-permute-start.9 = (bf16[144,3584]{1,0:T(8,128)(2,1)S(1)}, bf16[144,3584]{1,0:T(8,128)(2,1)S(1)}, u32[]{:S(2)}, u32[]{:S(2)}) collective-permute-start(bf16[144,3584]{1,0:T(8,128)(2,1)S(1)} %get-tuple-element.82.refs_0_), channel_id=1, source_target_pairs={{2,4},{4,6},{3,5},{5,7},{10,12},{12,14},{11,13},{13,15},{18,20},{2... | collective-permute-start | bytes 3096584 | tf_op jit(solution)/shard_map/ppermute | solution.py:387
  39.3 44.1 %collective-permute-start.10 = (bf16[144,3584]{1,0:T(8,128)(2,1)S(1)}, bf16[144,3584]{1,0:T(8,128)(2,1)S(1)}, u32[]{:S(2)}, u32[]{:S(2)}) collective-permute-start(bf16[144,3584]{1,0:T(8,128)(2,1)S(1)} %get-tuple-element.83.refs_1_), channel_id=1, source_target_pairs={{2,0},{4,2},{3,1},{5,3},{10,8},{12,10},{11,9},{13,11},{18,16},{20,... | collective-permute-start | bytes 3096584 | tf_op jit(solution)/shard_map/ppermute | solution.py:387
  43.3 41.2 %collective-permute-start.12 = (bf16[80,3584]{1,0:T(8,128)(2,1)S(1)}, bf16[80,3584]{1,0:T(8,128)(2,1)S(1)}, u32[]{:S(2)}, u32[]{:S(2)}) collective-permute-start(bf16[80,3584]{1,0:T(8,128)(2,1)S(1)} %get-tuple-element.86), channel_id=1, source_target_pairs={{0,16},{1,17},{8,24},{9,25},{16,0},{17,1},{24,8},{25,9},{2,18},{3,... | collective-permute-start | bytes 1720328 | tf_op jit(solution)/shard_map/ppermute | solution.py:41
  51.2 41.0 %collective-permute-start.13 = (bf16[80,3584]{1,0:T(8,128)(2,1)}, bf16[80,3584]{1,0:T(8,128)(2,1)}, u32[]{:S(2)}, u32[]{:S(2)}) collective-permute-start(bf16[80,3584]{1,0:T(8,128)(2,1)} %get-tuple-element.87), channel_id=1, source_target_pairs={{0,1},{1,0},{8,9},{9,8},{16,17},{17,16},{24,25},{25,24},{2,3},{3,2... | collective-permute-start | bytes 1720328 | tf_op jit(solution)/shard_map/ppermute | solution.py:41
  64.7 29.0 %collective-permute-start.14 = (bf16[80,3584]{1,0:T(8,128)(2,1)S(1)}, bf16[80,3584]{1,0:T(8,128)(2,1)}, u32[]{:S(2)}, u32[]{:S(2)}) collective-permute-start(bf16[80,3584]{1,0:T(8,128)(2,1)S(1)} %get-tuple-element.88), channel_id=1, source_target_pairs={{0,17},{1,16},{8,25},{9,24},{16,1},{17,0},{24,9},{25,8},{2,19},{3,... | collective-permute-start | bytes 1720328 | tf_op jit(solution)/shard_map/ppermute | solution.py:41
  84.5 26.7 %collective-permute-start.11 = (bf16[144,3584]{1,0:T(8,128)(2,1)S(1)}, bf16[144,3584]{1,0:T(8,128)(2,1)S(1)}, u32[]{:S(2)}, u32[]{:S(2)}) collective-permute-start(bf16[144,3584]{1,0:T(8,128)(2,1)S(1)} %get-tuple-element.84), channel_id=1, source_target_pairs={{2,0},{4,6},{3,1},{5,7},{10,8},{12,14},{11,9},{13,15},{18,16},{20,... | collective-permute-start | bytes 3096584 | tf_op jit(solution)/shard_map/ppermute | solution.py:458
  91.7 28.3 %collective-permute-start.23 = (bf16[80,3584]{1,0:T(8,128)(2,1)}, bf16[80,3584]{1,0:T(8,128)(2,1)}, u32[]{:S(2)}, u32[]{:S(2)}) collective-permute-start(bf16[80,3584]{1,0:T(8,128)(2,1)} %get-tuple-element.102), channel_id=1, source_target_pairs={{0,1},{1,0},{8,9},{9,8},{16,17},{17,16},{24,25},{25,24},{2,3},{3,2... | collective-permute-start | bytes 1720328 | tf_op jit(solution)/shard_map/ppermute | solution.py:41
  92.2 27.7 %collective-permute-start.24 = (bf16[80,3584]{1,0:T(8,128)(2,1)S(1)}, bf16[80,3584]{1,0:T(8,128)(2,1)}, u32[]{:S(2)}, u32[]{:S(2)}) collective-permute-start(bf16[80,3584]{1,0:T(8,128)(2,1)S(1)} %get-tuple-element.103), channel_id=1, source_target_pairs={{0,17},{1,16},{8,25},{9,24},{16,1},{17,0},{24,9},{25,8},{2,19},{3,... | collective-permute-start | bytes 1720328 | tf_op jit(solution)/shard_map/ppermute | solution.py:41
  118.0 24.3 %collective-permute-start.21 = (bf16[80,3584]{1,0:T(8,128)(2,1)S(1)}, bf16[80,3584]{1,0:T(8,128)(2,1)S(1)}, u32[]{:S(2)}, u32[]{:S(2)}) collective-permute-start(bf16[80,3584]{1,0:T(8,128)(2,1)S(1)} %get-tuple-element.99), channel_id=1, source_target_pairs={{0,1},{1,0},{8,9},{9,8},{16,17},{17,16},{24,25},{25,24},{2,3},{3,2... | collective-permute-start | bytes 1720328 | tf_op jit(solution)/shard_map/ppermute | solution.py:41
  118.5 27.7 %collective-permute-start.22 = (bf16[80,3584]{1,0:T(8,128)(2,1)S(1)}, bf16[80,3584]{1,0:T(8,128)(2,1)}, u32[]{:S(2)}, u32[]{:S(2)}) collective-permute-start(bf16[80,3584]{1,0:T(8,128)(2,1)S(1)} %get-tuple-element.100), channel_id=1, source_target_pairs={{0,17},{1,16},{8,25},{9,24},{16,1},{17,0},{24,9},{25,8},{2,19},{3,... | collective-permute-start | bytes 1720328 | tf_op jit(solution)/shard_map/ppermute | solution.py:41
  138.0 27.5 %collective-permute-start.28 = (bf16[80,3584]{1,0:T(8,128)(2,1)S(1)}, bf16[80,3584]{1,0:T(8,128)(2,1)S(1)}, u32[]{:S(2)}, u32[]{:S(2)}) collective-permute-start(bf16[80,3584]{1,0:T(8,128)(2,1)S(1)} %get-tuple-element.112), channel_id=1, source_target_pairs={{0,16},{1,17},{8,24},{9,25},{16,0},{17,1},{24,8},{25,9},{2,18},{3,... | collective-permute-start | bytes 1720328 | tf_op jit(solution)/shard_map/ppermute | solution.py:41
  139.6 27.5 %collective-permute-start.29 = (bf16[80,3584]{1,0:T(8,128)(2,1)S(1)}, bf16[80,3584]{1,0:T(8,128)(2,1)S(1)}, u32[]{:S(2)}, u32[]{:S(2)}) collective-permute-start(bf16[80,3584]{1,0:T(8,128)(2,1)S(1)} %get-tuple-element.113), channel_id=1, source_target_pairs={{0,1},{1,0},{8,9},{9,8},{16,17},{17,16},{24,25},{25,24},{2,3},{3,2... | collective-permute-start | bytes 1720328 | tf_op jit(solution)/shard_map/ppermute | solution.py:41
  140.9 29.9 %collective-permute-start.30 = (bf16[80,3584]{1,0:T(8,128)(2,1)}, bf16[80,3584]{1,0:T(8,128)(2,1)S(1)}, u32[]{:S(2)}, u32[]{:S(2)}) collective-permute-start(bf16[80,3584]{1,0:T(8,128)(2,1)} %get-tuple-element.114), channel_id=1, source_target_pairs={{0,17},{1,16},{8,25},{9,24},{16,1},{17,0},{24,9},{25,8},{2,19},{3,... | collective-permute-start | bytes 1720328 | tf_op jit(solution)/shard_map/ppermute | solution.py:41
  165.6 28.6 %collective-permute-start.27 = (bf16[80,3584]{1,0:T(8,128)(2,1)}, bf16[80,3584]{1,0:T(8,128)(2,1)S(1)}, u32[]{:S(2)}, u32[]{:S(2)}) collective-permute-start(bf16[80,3584]{1,0:T(8,128)(2,1)} %get-tuple-element.108), channel_id=1, source_target_pairs={{0,17},{1,16},{8,25},{9,24},{16,1},{17,0},{24,9},{25,8},{2,19},{3,... | collective-permute-start | bytes 1720328 | tf_op jit(solution)/shard_map/ppermute | solution.py:41
  175.1 44.8 %collective-permute-start.34 = (bf16[128,3584]{1,0:T(8,128)(2,1)S(1)}, bf16[128,3584]{1,0:T(8,128)(2,1)S(1)}, u32[]{:S(2)}, u32[]{:S(2)}) collective-permute-start(bf16[128,3584]{1,0:T(8,128)(2,1)S(1)} %shard_map.85.refs_4_), channel_id=1, source_target_pairs={{0,4},{2,6},{4,0},{6,2},{1,5},{3,7},{5,1},{7,3},{8,12},{10,14},{12... | collective-permute-start | bytes 2752520 | tf_op jit(solution)/shard_map/ppermute | solution.py:29
  196.0 25.7 %collective-permute-start.38 = (bf16[80,3584]{1,0:T(8,128)(2,1)S(1)}, bf16[80,3584]{1,0:T(8,128)(2,1)S(1)}, u32[]{:S(2)}, u32[]{:S(2)}) collective-permute-start(bf16[80,3584]{1,0:T(8,128)(2,1)S(1)} %get-tuple-element.126), channel_id=1, source_target_pairs={{0,16},{1,17},{8,24},{9,25},{16,0},{17,1},{24,8},{25,9},{2,18},{3,... | collective-permute-start | bytes 1720328 | tf_op jit(solution)/shard_map/ppermute | solution.py:41
  197.6 24.1 %collective-permute-start.39 = (bf16[80,3584]{1,0:T(8,128)(2,1)S(1)}, bf16[80,3584]{1,0:T(8,128)(2,1)S(1)}, u32[]{:S(2)}, u32[]{:S(2)}) collective-permute-start(bf16[80,3584]{1,0:T(8,128)(2,1)S(1)} %get-tuple-element.127), channel_id=1, source_target_pairs={{0,1},{1,0},{8,9},{9,8},{16,17},{17,16},{24,25},{25,24},{2,3},{3,2... | collective-permute-start | bytes 1720328 | tf_op jit(solution)/shard_map/ppermute | solution.py:41
  198.2 26.7 %collective-permute-start.40 = (bf16[80,3584]{1,0:T(8,128)(2,1)S(1)}, bf16[80,3584]{1,0:T(8,128)(2,1)S(1)}, u32[]{:S(2)}, u32[]{:S(2)}) collective-permute-start(bf16[80,3584]{1,0:T(8,128)(2,1)S(1)} %get-tuple-element.128), channel_id=1, source_target_pairs={{0,17},{1,16},{8,25},{9,24},{16,1},{17,0},{24,9},{25,8},{2,19},{3,... | collective-permute-start | bytes 1720328 | tf_op jit(solution)/shard_map/ppermute | solution.py:41
  227.2 25.7 %collective-permute-start.41 = (bf16[128,3584]{1,0:T(8,128)(2,1)S(1)}, bf16[128,3584]{1,0:T(8,128)(2,1)S(1)}, u32[]{:S(2)}, u32[]{:S(2)}) collective-permute-start(bf16[128,3584]{1,0:T(8,128)(2,1)S(1)} %shard_map.89.refs_4_), channel_id=1, source_target_pairs={{0,6},{2,4},{4,2},{6,0},{1,7},{3,5},{5,3},{7,1},{8,14},{10,12},{12... | collective-permute-start | bytes 2752520 | tf_op jit(solution)/shard_map/ppermute | solution.py:29
  233.7 26.1 %collective-permute-start.37 = (bf16[80,3584]{1,0:T(8,128)(2,1)S(1)}, bf16[80,3584]{1,0:T(8,128)(2,1)S(1)}, u32[]{:S(2)}, u32[]{:S(2)}) collective-permute-start(bf16[80,3584]{1,0:T(8,128)(2,1)S(1)} %get-tuple-element.125), channel_id=1, source_target_pairs={{0,17},{1,16},{8,25},{9,24},{16,1},{17,0},{24,9},{25,8},{2,19},{3,... | collective-permute-start | bytes 1720328 | tf_op jit(solution)/shard_map/ppermute | solution.py:41
  235.3 36.7 %collective-permute-start.46 = (bf16[128,3584]{1,0:T(8,128)(2,1)S(1)}, bf16[128,3584]{1,0:T(8,128)(2,1)S(1)}, u32[]{:S(2)}, u32[]{:S(2)}) collective-permute-start(bf16[128,3584]{1,0:T(8,128)(2,1)S(1)} %add_convert_fusion.1), channel_id=1, source_target_pairs={{0,2},{2,0},{4,6},{6,4},{1,3},{3,1},{5,7},{7,5},{8,10},{10,8},{12,... | collective-permute-start | bytes 2752520 | tf_op jit(solution)/shard_map/ppermute | solution.py:29
  (39 other events, 433.1 us)
